TPU v7x, 256 devices: a whole 4x4x8 slice. The times are simulated.
256 devices in a mesh: gx: 16 (over x, z_lo), gy: 16 (over y, z_hi, core).
Axes of the slice: x: 4, y: 4, z: 8 (z_hi: 2, z_lo: 4; z = z_hi * 4 + z_lo), core: 2. Of those that a mesh axis runs over, the one named last changes fastest.
Arguments:
- images: float32 [1024, 128, 2048], P(None, 'gx', 'gy'), may hold values from 0 to 600, as said below
Outputs:
- colocal: float32 [1024, 1024], P(('gx', 'gy'))
Inputs may be any that keep to these rules, and one draw needn't show every extreme that they name: `images`: intensities are non-negative.
All inputs are finite; a program needn't handle non-finite values.
Results may differ from a plain program's by a relative error of at most 0.00035.
Values sent between devices are 32-bit elements; how exact they have to be, the bound alone decides.
No kernel may reach another device: no remote copies, remote signals or barrier semaphores. Data moves between devices by JAX's collectives and lax.ppermute only.
A program may use at most 128 MiB of HBM per device.

v0:
```python
import functools
import math

import jax
import jax.numpy as jnp
from jax import lax
from jax.experimental import pallas as pl
from jax.experimental.pallas import tpu as pltpu
from jax.sharding import Mesh, PartitionSpec as P

f32 = jnp.float32
HI = lax.Precision.HIGHEST
NT = (((1,), (1,)), ((), ()))
TILE = 8 * 128
PARTS = (
    ((0, 0), (0, 1), (1, 0), (1, 1)),
    ((2, 0), (2, 1), (2, 2), (0, 2), (1, 2)),
    ((3, 0), (3, 1), (3, 2), (3, 3), (0, 3), (1, 3), (2, 3)),
)
GX, GY = ("x", "zl"), ("y", "zh", "c")
AXES = GX + GY


def stencil_taps():
    raw = [math.exp(-k * k / 4.5) for k in range(-4, 5)]
    total = sum(raw)
    return [value / total for value in raw]


TAPS = stencil_taps()


def survey(x_ref, left_ref, right_ref):
    lane = lax.broadcasted_iota(jnp.int32, (64, 128), 1)
    left = jnp.zeros((64, 128), f32)
    right = jnp.zeros((64, 128), f32)
    for g in range(4):
        for r in range(8):
            row = x_ref[g, pl.ds(r, 64, stride=8), :]
            slot = g * 32 + r * 4
            here = (lane >= slot) & (lane < slot + 4)
            left = jnp.where(here, pltpu.roll(row, slot, 1) if slot else row, left)
            right = jnp.where(here, pltpu.roll(row, (slot + 4) % 128, 1), right)
    left_ref[...] = left
    right_ref[...] = right


def build_weights(order_ref, w_ref):
    at = lax.broadcasted_iota(jnp.int32, (128, 128), 0)
    col = lax.broadcasted_iota(jnp.int32, (128, 128), 1)

    def taps(distance):
        value = jnp.zeros((128, 128), f32)
        for k in range(5):
            value = jnp.where(distance == k, f32(TAPS[4 + k]), value)
        return value

    band = taps(jnp.abs(at - col))
    halo = taps(jnp.abs(at % 4 + jnp.where(at < 32, -4, 128) - col))
    for r in range(8):
        w_ref[r, 0:128] = band
        w_ref[r, 128:256] = jnp.where((at < 64) & (at % 32 // 4 == r), halo, 0.0)


def halo_lanes(g, left, right):
    lane = lax.broadcasted_iota(jnp.int32, left.shape, 1)
    left = pltpu.roll(left, (128 - 32 * g) % 128, 1) if g else left
    right = pltpu.roll(right, (160 - 32 * g) % 128, 1) if g != 1 else right
    return jnp.where(lane < 32, left, jnp.where(lane < 64, right, 0.0))


def smooth_row(row, halo, w):
    wide = jnp.concatenate([row, halo], axis=1)
    return jnp.dot(wide, w, precision=HI, preferred_element_type=f32)


def row_pass(group, count, x_ref, left_ref, right_ref, w_ref, order_ref, top_ref, bot_ref):
    for part in range(2 * count):
        at = slice(part * 128, (part + 1) * 128)
        edge = slice(part % 2 * 128, part % 2 * 128 + 128)
        halo = halo_lanes(group + part // 2, left_ref[edge], right_ref[edge])
        for r in range(8):
            smooth = smooth_row(x_ref[2 * group + part, pl.ds(r, 128, stride=8), :], halo, w_ref[r])
            if r < 4:
                top_ref[r, at] = smooth
            else:
                bot_ref[r - 4, at] = smooth


def to_lanes(squares, level):
    ones = jnp.ones((8, 128), f32)
    pick = jnp.where(lax.broadcasted_iota(jnp.int32, (8, 128), 1) == 0, f32(1), f32(0))
    spread = lax.dot_general(ones, squares, NT, precision=HI, preferred_element_type=f32)
    mean = lax.dot_general(pick, level, NT, precision=HI, preferred_element_type=f32)
    return spread[0:1], mean[0:1]


def smooth_down(rows):
    smooth = []
    for r in range(8):
        v = rows[r + 4] * TAPS[4]
        for k in range(1, 5):
            v = v + (rows[r + 4 - k] + rows[r + 4 + k]) * TAPS[4 + k]
        smooth.append(v)
    return smooth


def column_pass(above_ref, top_ref, bot_ref, below_ref, *refs):
    u_ref, spread_ref, mean_ref, square_ref, level_ref = refs[-5:]

    def step(s, carry):
        at = pl.ds(pl.multiple_of(s * 16, 16), 16)
        smooth = smooth_down([ref[i, at, :] for ref in (above_ref, top_ref, bot_ref, below_ref) for i in range(4)])
        total = ((smooth[0] + smooth[1]) + (smooth[2] + smooth[3])) + ((smooth[4] + smooth[5]) + (smooth[6] + smooth[7]))
        mean = jnp.sum(total, axis=1, keepdims=True) * f32(1.0 / TILE)
        acc = jnp.zeros((16, 128), f32)
        for r in range(8):
            centered = smooth[r] - mean
            acc = acc + centered * centered
            u_ref[at, r * 128:(r + 1) * 128] = centered.astype(jnp.bfloat16)
        square_ref[at, :] = acc
        level_ref[at, :] = jnp.broadcast_to(mean, (16, 128))
        return carry

    lax.fori_loop(0, square_ref.shape[0] // 16, step, 0, unroll=4)
    spread_ref[...], mean_ref[...] = to_lanes(square_ref[...], level_ref[...])


def gram(blocks, *refs):
    count = 1 + max(a for a, b in blocks)
    units, refs = refs[:count], refs[count:]
    vectors, (keep_ref, send_ref) = refs[:-2], refs[-2:]
    first = lax.axis_index("c") == 0
    sub = lax.broadcasted_iota(jnp.int32, (8, 128), 0)
    for n, (row, col) in enumerate(blocks):
        part = lax.dot_general(units[row][...], units[col][...], NT, preferred_element_type=f32)
        for zl in range(4):
            for y in range(4):
                at = (zl * 4 + y) * 16
                for cb in range(2):
                    a = part[at:at + 8, cb * 128:(cb + 1) * 128]
                    b = part[at + 8:at + 16, cb * 128:(cb + 1) * 128]
                    c0 = jnp.where(sub < 4, a, pltpu.roll(b, 4, 0))
                    c1 = jnp.where(sub < 4, pltpu.roll(a, 4, 0), b)
                    keep_ref[y, n * 8 + zl * 2 + cb] = jnp.where(first, c0, c1)
                    send_ref[y, n * 8 + zl * 2 + cb] = jnp.where(first, c1, c0)
    if vectors:
        spread_ref, mean_ref = vectors
        end = len(blocks) * 8
        for y in range(4):
            for ref, own, other in ((keep_ref, 1, 2), (send_ref, 2, 1)):
                ref[y, end] = spread_ref[...]
                ref[y, end + own] = mean_ref[...]
                ref[y, end + other] = jnp.zeros((8, 128), f32)


def merge(*refs):
    parts, out_ref = refs[:-1], refs[-1]
    for q, blocks in enumerate(PARTS):
        keep, other = parts[2 * q:2 * q + 2]
        for n, (row, col) in enumerate(blocks):
            for y in range(4):
                for zl in range(4):
                    at, to = n * 8 + zl * 2, zl * 8 + col * 2
                    out_ref[row * 4 + y, to:to + 2] = keep[y, at:at + 2] + other[y, at:at + 2]
    keep, other = parts[-2:]
    end = len(PARTS[-1]) * 8
    for x in range(4):
        for y in range(4):
            out_ref[x * 4 + y, 32:35] = keep[y, end:end + 3] + other[y, end:end + 3]


def between(shift_ref, select):
    wide = jnp.concatenate([shift_ref[cb] for cb in range(8)], axis=1)
    rows = [
        lax.dot_general(one_hot, shift_ref[block], NT, precision=HI, preferred_element_type=f32)
        for block, one_hot in select
    ]
    rows = jnp.concatenate(rows, axis=0) if len(rows) > 1 else rows[0]
    return jnp.dot(rows, wide, precision=HI, preferred_element_type=f32)


def fold(part_ref, out_ref, shift_ref):
    x, y, c = lax.axis_index("x"), lax.axis_index("y"), lax.axis_index("c")
    sub = lax.broadcasted_iota(jnp.int32, (8, 128), 0)
    lane = lax.broadcasted_iota(jnp.int32, (8, 128), 1)

    def summed(t):
        s = part_ref[0, t]
        for p in range(1, 16):
            s = s + part_ref[p, t]
        return s

    mean = (summed(33) + summed(34)) * f32(1.0 / 32)
    spread = summed(32)
    for k in range(2):
        for p in range(16):
            shift = part_ref[p, 33 + k] - mean
            spread = spread + shift * shift * f32(TILE)
            for cb in range(8):
                shift_ref[cb, k * 16 + p:k * 16 + p + 1, :] = shift[cb:cb + 1]
    select = []
    for zl in range(4):
        want = (zl % 2) * 64 + y * 16 + (sub // 4) * 8 + c * 4 + sub % 4
        select.append((2 * x + zl // 2, jnp.where(lane == want, f32(1), f32(0))))
    extra = between(shift_ref, select) * f32(TILE)
    for zl in range(4):
        for k in range(4):
            a, b = [
                summed(zl * 8 + cb) + extra[zl * 8:zl * 8 + 8, cb * 128:(cb + 1) * 128] for cb in (2 * k, 2 * k + 1)
            ]
            out_ref[zl * 2, k] = jnp.where(sub < 4, a, pltpu.roll(b, 4, 0))
            out_ref[zl * 2 + 1, k] = jnp.where(sub < 4, pltpu.roll(a, 4, 0), b)
        for zh in range(2):
            out_ref[zl * 2 + zh, 4] = spread
            out_ref[zl * 2 + zh, 5] = mean


def finish(part_ref, out_ref, shift_ref):
    first_row = lax.axis_index(AXES) * 4
    sub = lax.broadcasted_iota(jnp.int32, (8, 128), 0)
    lane = lax.broadcasted_iota(jnp.int32, (8, 128), 1)

    def summed(t):
        s = part_ref[0, t]
        for p in range(1, 8):
            s = s + part_ref[p, t]
        return s

    mean = summed(5) * f32(1.0 / 8)
    spread = summed(4)
    for p in range(8):
        shift = part_ref[p, 5] - mean
        spread = spread + shift * shift * f32(32 * TILE)
        for cb in range(8):
            shift_ref[cb, p:p + 1, :] = shift[cb:cb + 1]
    one_hot = jnp.where(lane == first_row % 128 + sub % 4, f32(1), f32(0))
    extra = between(shift_ref, [(first_row // 128, one_hot)]) * f32(32 * TILE)
    scale = 1.0 / jnp.sqrt(spread + 1e-06)
    flat = sub * 128 + lane
    own = jnp.zeros((8, 128), f32)
    for i in range(4):
        value = jnp.sum(jnp.where(flat == first_row + i, scale, 0.0))
        own = jnp.where((sub & 3) == i, value, own)
    for k in range(4):
        at, to = 2 * k * 128, (2 * k + 1) * 128
        cols = jnp.where(sub < 4, scale[2 * k:2 * k + 1, :], scale[2 * k + 1:2 * k + 2, :])
        more = jnp.where(sub < 4, extra[:, at:to], extra[:, to:to + 128])
        tile = (summed(k) + more) * cols * own
        out_ref[:, at:to] = tile[0:4]
        out_ref[:, to:to + 128] = tile[4:8]


def local(images):
    shape = jax.ShapeDtypeStruct
    vmem = pl.BlockSpec(memory_space=pltpu.VMEM)
    anywhere = pl.BlockSpec(memory_space=pl.ANY)
    params = pltpu.CompilerParams(vmem_limit_bytes=48 * 1024 * 1024)
    by_group = images.reshape(4, 2048, 128)
    by_eighth = images.reshape(8, 1024, 128)
    up = [(i, i + 1) for i in range(15)]
    down = [(j, i) for i, j in up]
    edge_shape = [shape((256, 128), f32)] * 2

    def unit_shape(count):
        return [shape((count, 1024), jnp.bfloat16), shape((1, count), f32), shape((1, count), f32)]

    def swap(axes, ahead, back):
        return lax.ppermute(ahead, axes, up), lax.ppermute(back, axes, down)

    left, right = pl.pallas_call(
        survey,
        grid=(4,),
        in_specs=[pl.BlockSpec((4, 512, 128), lambda i: (0, i, 0))],
        out_specs=[pl.BlockSpec((64, 128), lambda i: (i, 0))] * 2,
        out_shape=edge_shape,
        compiler_params=params,
    )(by_group)
    edges = swap(GY, right, left)
    weights = pl.pallas_call(
        build_weights,
        in_specs=[anywhere],
        out_specs=vmem,
        out_shape=shape((8, 256, 128), f32),
        compiler_params=params,
    )(left)

    def smooth_rows(group, count, order):
        top, bot = pl.pallas_call(
            functools.partial(row_pass, group, count),
            in_specs=[vmem] * 4 + [anywhere],
            out_specs=[vmem] * 2,
            out_shape=[shape((4, 256 * count, 128), f32)] * 2,
            compiler_params=params,
        )(by_eighth, *edges, weights, order)
        above, below = swap(GX, bot, top)
        return above, top, bot, below

    chunks = []
    for group, count in [(0, 1), (1, 1), (2, 1), (3, 1)]:
        chunks.append(smooth_rows(group, count, chunks[-1][1] if chunks else left))
    units, spreads, means, parts = [], [], [], []
    order = [left]
    for q, sources in enumerate(chunks):
        unit, spread, mean = pl.pallas_call(
            column_pass,
            in_specs=[vmem] * 4 + [anywhere] * len(order),
            out_specs=[vmem] * 3,
            out_shape=unit_shape(256),
            scratch_shapes=[pltpu.VMEM((256, 128), f32)] * 2,
            compiler_params=params,
        )(*sources, *order)
        units.append(unit)
        spreads.append(spread)
        means.append(mean)
        order = [unit]
        if q == 0:
            continue
        blocks = PARTS[q - 1]
        vectors = []
        if q == 3:
            vectors = [jnp.concatenate(v, axis=1).reshape(8, 128) for v in (spreads, means)]
        tiles = len(blocks) * 8 + (3 if vectors else 0)
        keep, send = pl.pallas_call(
            functools.partial(gram, blocks),
            in_specs=[vmem] * (len(units) + len(vectors)),
            out_specs=[vmem] * 2,
            out_shape=[shape((4, tiles, 8, 128), f32)] * 2,
            compiler_params=params,
        )(*units, *vectors)
        parts += [keep, lax.ppermute(send, "c", [(0, 1), (1, 0)])]
        order = [keep, parts[1]] if q == 2 else [keep]

    part = pl.pallas_call(
        merge,
        in_specs=[vmem] * 6,
        out_specs=vmem,
        out_shape=shape((16, 35, 8, 128), f32),
        compiler_params=params,
    )(*parts)
    part = lax.all_to_all(part, ("x", "y"), 0, 0, tiled=True)
    part = pl.pallas_call(
        fold,
        in_specs=[vmem],
        out_specs=vmem,
        out_shape=shape((8, 6, 8, 128), f32),
        scratch_shapes=[pltpu.VMEM((8, 32, 128), f32)],
        compiler_params=params,
    )(part)
    part = lax.all_to_all(part, ("zl", "zh"), 0, 0, tiled=True)
    return pl.pallas_call(
        finish,
        in_specs=[vmem],
        out_specs=vmem,
        out_shape=shape((4, 1024), f32),
        scratch_shapes=[pltpu.VMEM((8, 8, 128), f32)],
        compiler_params=params,
    )(part)


def solution(mesh):
    fine = Mesh(mesh.devices.reshape(4, 4, 4, 2, 2), AXES)
    return jax.shard_map(
        local,
        mesh=fine,
        in_specs=(P(None, GX, GY),),
        out_specs=P(AXES, None),
        check_vma=False,
    )
```

profile of v0, /device:TPU:32, one launch (start us, length us, event | category | flops | bytes accessed | tf_op | source)
XLA Modules:
  0.0 182.2 jit_solution(13636767120126927057)
XLA Ops:
  0.0 0.0 copy-start
  0.0 2.2 %copy-done = f32[1024,8,128]{2,1,0:T(8,128)S(1)} copy-done((f32[1024,8,128]{2,1,0:T(8,128)S(1)}, f32[1024,8,128]{2,1,0:T(8,128)}, u32[]{:S(2)}) %copy-start) | copy-done | bytes 4194328
  2.2 2.8 %shard_map.17 = (f32[256,128]{1,0:T(8,128)S(1)}, f32[256,128]{1,0:T(8,128)S(1)}) custom-call(f32[4,2048,128]{2,1,0:T(8,128)S(1)} %bitcast.8), custom_call_target="tpu_custom_call" | custom-call | tf_op jit(solution)/shard_map/pallas_call | solution.py:271
  5.0 1.7 collective-permute-start
  6.8 1.3 collective-permute-start.1
  8.1 0.1 shard_map.18.w_ref
  8.1 0.0 collective-permute-done.left_ref
  8.2 7.9 %collective-permute-done.1.right_ref = f32[256,128]{1,0:T(8,128)S(1)} collective-permute-done((f32[256,128]{1,0:T(8,128)S(1)}, f32[256,128]{1,0:T(8,128)S(1)}, u32[]{:S(2)}, u32[]{:S(2)}) %collective-permute-start.1) | collective-permute-done | bytes 131104 | tf_op jit(solution)/shard_map/ppermute | solution.py:269
  16.1 4.1 %shard_map.19 = (f32[4,256,128]{2,1,0:T(8,128)S(1)}, f32[4,256,128]{2,1,0:T(8,128)S(1)}) custom-call(f32[8,1024,128]{2,1,0:T(8,128)} %bitcast.4, f32[256,128]{1,0:T(8,128)S(1)} %collective-permute-done.left_ref, f32[256,128]{1,0:T(8,128)S(1)} %collective-permute-done.1.right_ref, f32[8,256,128]{2,1,0:T(8,128)S(1)} %shard_map.18.w_ref, ...), custom_call_target="tpu_custom_call" | custom-call | tf_op jit(solution)/shard_map/pallas_call | solution.py:289
  20.2 2.9 %collective-permute-start.2 = (f32[4,256,128]{2,1,0:T(8,128)S(1)}, f32[4,256,128]{2,1,0:T(8,128)S(1)}, u32[]{:S(2)}, u32[]{:S(2)}) collective-permute-start(f32[4,256,128]{2,1,0:T(8,128)S(1)} %get-tuple-element.35.bot_ref), channel_id=1, source_target_pairs={{0,16},{16,32},{32,48},{48,64},{64,80},{80,96},{96,112},{112,128},... | collective-permute-start | bytes 1572872 | tf_op jit(solution)/shard_map/ppermute | solution.py:269
  23.1 2.9 %collective-permute-start.3 = (f32[4,256,128]{2,1,0:T(8,128)S(1)}, f32[4,256,128]{2,1,0:T(8,128)S(1)}, u32[]{:S(2)}, u32[]{:S(2)}) collective-permute-start(f32[4,256,128]{2,1,0:T(8,128)S(1)} %get-tuple-element.36.top_ref.order_ref), channel_id=1, source_target_pairs={{16,0},{32,16},{48,32},{64,48},{80,64},{96,80},{112,96},{128,112},... | collective-permute-start | bytes 1572872 | tf_op jit(solution)/shard_map/ppermute | solution.py:269
  26.1 4.1 %shard_map.21 = (f32[4,256,128]{2,1,0:T(8,128)S(1)}, f32[4,256,128]{2,1,0:T(8,128)S(1)}) custom-call(f32[8,1024,128]{2,1,0:T(8,128)} %bitcast.5, f32[256,128]{1,0:T(8,128)S(1)} %collective-permute-done.left_ref, f32[256,128]{1,0:T(8,128)S(1)} %collective-permute-done.1.right_ref, f32[8,256,128]{2,1,0:T(8,128)S(1)} %shard_map.18.w_ref, ...), custom_call_target="tpu_custom_call" | custom-call | tf_op jit(solution)/shard_map/pallas_call | solution.py:289
  30.2 2.9 %collective-permute-start.4 = (f32[4,256,128]{2,1,0:T(8,128)S(1)}, f32[4,256,128]{2,1,0:T(8,128)S(1)}, u32[]{:S(2)}, u32[]{:S(2)}) collective-permute-start(f32[4,256,128]{2,1,0:T(8,128)S(1)} %get-tuple-element.38.bot_ref), channel_id=1, source_target_pairs={{0,16},{16,32},{32,48},{48,64},{64,80},{80,96},{96,112},{112,128},... | collective-permute-start | bytes 1572872 | tf_op jit(solution)/shard_map/ppermute | solution.py:269
  33.1 3.0 %collective-permute-start.5 = (f32[4,256,128]{2,1,0:T(8,128)S(1)}, f32[4,256,128]{2,1,0:T(8,128)S(1)}, u32[]{:S(2)}, u32[]{:S(2)}) collective-permute-start(f32[4,256,128]{2,1,0:T(8,128)S(1)} %get-tuple-element.39.top_ref.order_ref), channel_id=1, source_target_pairs={{16,0},{32,16},{48,32},{64,48},{80,64},{96,80},{112,96},{128,112},... | collective-permute-start | bytes 1572872 | tf_op jit(solution)/shard_map/ppermute | solution.py:269
  36.1 4.1 %shard_map.24 = (f32[4,256,128]{2,1,0:T(8,128)S(1)}, f32[4,256,128]{2,1,0:T(8,128)S(1)}) custom-call(f32[8,1024,128]{2,1,0:T(8,128)} %bitcast.6, f32[256,128]{1,0:T(8,128)S(1)} %collective-permute-done.left_ref, f32[256,128]{1,0:T(8,128)S(1)} %collective-permute-done.1.right_ref, f32[8,256,128]{2,1,0:T(8,128)S(1)} %shard_map.18.w_ref, ...), custom_call_target="tpu_custom_call" | custom-call | tf_op jit(solution)/shard_map/pallas_call | solution.py:289
  40.2 1.9 %collective-permute-start.8 = (f32[4,256,128]{2,1,0:T(8,128)S(1)}, f32[4,256,128]{2,1,0:T(8,128)S(1)}, u32[]{:S(2)}, u32[]{:S(2)}) collective-permute-start(f32[4,256,128]{2,1,0:T(8,128)S(1)} %get-tuple-element.44.top_ref.order_ref), channel_id=1, source_target_pairs={{16,0},{32,16},{48,32},{64,48},{80,64},{96,80},{112,96},{128,112},... | collective-permute-start | bytes 1572872 | tf_op jit(solution)/shard_map/ppermute | solution.py:269
  42.1 4.1 %shard_map.27 = (f32[4,256,128]{2,1,0:T(8,128)S(1)}, f32[4,256,128]{2,1,0:T(8,128)S(1)}) custom-call(f32[8,1024,128]{2,1,0:T(8,128)} %bitcast.7, f32[256,128]{1,0:T(8,128)S(1)} %collective-permute-done.left_ref, f32[256,128]{1,0:T(8,128)S(1)} %collective-permute-done.1.right_ref, f32[8,256,128]{2,1,0:T(8,128)S(1)} %shard_map.18.w_ref, ...), custom_call_target="tpu_custom_call" | custom-call | tf_op jit(solution)/shard_map/pallas_call | solution.py:289
  46.3 0.0 collective-permute-done.2.above_ref
  46.3 3.9 %collective-permute-start.10 = (f32[4,256,128]{2,1,0:T(8,128)S(1)}, f32[4,256,128]{2,1,0:T(8,128)S(1)}, u32[]{:S(2)}, u32[]{:S(2)}) collective-permute-start(f32[4,256,128]{2,1,0:T(8,128)S(1)} %get-tuple-element.48.bot_ref), channel_id=1, source_target_pairs={{0,16},{16,32},{32,48},{48,64},{64,80},{80,96},{96,112},{112,128},... | collective-permute-start | bytes 1572872 | tf_op jit(solution)/shard_map/ppermute | solution.py:269
  50.2 2.9 %collective-permute-done.3.below_ref = f32[4,256,128]{2,1,0:T(8,128)S(1)} collective-permute-done((f32[4,256,128]{2,1,0:T(8,128)S(1)}, f32[4,256,128]{2,1,0:T(8,128)S(1)}, u32[]{:S(2)}, u32[]{:S(2)}) %collective-permute-start.3) | collective-permute-done | bytes 524320 | tf_op jit(solution)/shard_map/ppermute | solution.py:269
  53.1 2.5 %collective-permute-start.7 = (f32[4,256,128]{2,1,0:T(8,128)S(1)}, f32[4,256,128]{2,1,0:T(8,128)S(1)}, u32[]{:S(2)}, u32[]{:S(2)}) collective-permute-start(f32[4,256,128]{2,1,0:T(8,128)S(1)} %get-tuple-element.43.bot_ref), channel_id=1, source_target_pairs={{0,16},{16,32},{32,48},{48,64},{64,80},{80,96},{96,112},{112,128},... | collective-permute-start | bytes 1572872 | tf_op jit(solution)/shard_map/ppermute | solution.py:269
  55.6 1.2 shard_map.20
  56.8 0.0 collective-permute-done.4.above_ref
  56.8 3.4 %collective-permute-start.11 = (f32[4,256,128]{2,1,0:T(8,128)S(1)}, f32[4,256,128]{2,1,0:T(8,128)S(1)}, u32[]{:S(2)}, u32[]{:S(2)}) collective-permute-start(f32[4,256,128]{2,1,0:T(8,128)S(1)} %get-tuple-element.49.top_ref), channel_id=1, source_target_pairs={{16,0},{32,16},{48,32},{64,48},{80,64},{96,80},{112,96},{128,112},... | collective-permute-start | bytes 1572872 | tf_op jit(solution)/shard_map/ppermute | solution.py:269
  60.1 10.8 %collective-permute-done.5.below_ref = f32[4,256,128]{2,1,0:T(8,128)S(1)} collective-permute-done((f32[4,256,128]{2,1,0:T(8,128)S(1)}, f32[4,256,128]{2,1,0:T(8,128)S(1)}, u32[]{:S(2)}, u32[]{:S(2)}) %collective-permute-start.5) | collective-permute-done | bytes 524320 | tf_op jit(solution)/shard_map/ppermute | solution.py:269
  71.0 1.2 shard_map.22
  72.1 0.8 shard_map.23
  72.9 4.2 %collective-permute-start.6 = (f32[4,32,8,128]{3,2,1,0:T(8,128)S(1)}, f32[4,32,8,128]{3,2,1,0:T(8,128)S(1)}, u32[]{:S(2)}, u32[]{:S(2)}) collective-permute-start(f32[4,32,8,128]{3,2,1,0:T(8,128)S(1)} %get-tuple-element.42), channel_id=1, source_target_pairs={{0,1},{1,0},{2,3},{3,2},{4,5},{5,4},{6,7},{7,6},{8,9},{9,8},{10,11... | collective-permute-start | bytes 1572872 | tf_op jit(solution)/shard_map/ppermute | solution.py:331
  77.1 0.0 collective-permute-done.7.above_ref
  77.1 9.7 %collective-permute-done.8.below_ref = f32[4,256,128]{2,1,0:T(8,128)S(1)} collective-permute-done((f32[4,256,128]{2,1,0:T(8,128)S(1)}, f32[4,256,128]{2,1,0:T(8,128)S(1)}, u32[]{:S(2)}, u32[]{:S(2)}) %collective-permute-start.8) | collective-permute-done | bytes 524320 | tf_op jit(solution)/shard_map/ppermute | solution.py:269
  86.8 1.2 shard_map.25
  88.0 0.9 shard_map.26
  88.9 0.0 collective-permute-done.10.above_ref
  88.9 27.0 %collective-permute-done.11.below_ref = f32[4,256,128]{2,1,0:T(8,128)S(1)} collective-permute-done((f32[4,256,128]{2,1,0:T(8,128)S(1)}, f32[4,256,128]{2,1,0:T(8,128)S(1)}, u32[]{:S(2)}, u32[]{:S(2)}) %collective-permute-start.11) | collective-permute-done | bytes 524320 | tf_op jit(solution)/shard_map/ppermute | solution.py:269
  115.9 0.0 collective-permute-done.6.refs_1_
  115.9 1.2 shard_map.28
  117.1 1.2 shard_map.29
  118.2 1.8 collective-permute-start.12
  120.1 0.1 collective-permute-start.9
  120.2 3.0 %collective-permute-done.9.refs_3_ = f32[4,40,8,128]{3,2,1,0:T(8,128)S(1)} collective-permute-done((f32[4,40,8,128]{3,2,1,0:T(8,128)S(1)}, f32[4,40,8,128]{3,2,1,0:T(8,128)S(1)}, u32[]{:S(2)}, u32[]{:S(2)}) %collective-permute-start.9) | collective-permute-done | bytes 655392 | tf_op jit(solution)/shard_map/ppermute | solution.py:331
  123.2 0.0 collective-permute-done.12.refs_5_
  123.2 1.7 shard_map.30
  124.8 40.6 %all_to_all.10.part_ref = f32[16,35,8,128]{3,2,1,0:T(8,128)S(1)} all-to-all(f32[16,35,8,128]{3,2,1,0:T(8,128)} %shard_map.30), channel_id=1, replica_groups=mesh['x'=4,'zl'=4,'y'=4,'zh'=2,'c'=2] {'x','y'}, dimensions={0} | all-to-all | bytes 4587520 | tf_op jit(solution)/shard_map/all_to_all | solution.py:341
  165.5 0.6 shard_map.31
  166.0 15.2 %all_to_all.11.part_ref = f32[8,6,8,128]{3,2,1,0:T(8,128)S(1)} all-to-all(f32[8,6,8,128]{3,2,1,0:T(8,128)S(1)} %shard_map.31), channel_id=1, replica_groups=mesh['x'=4,'zl'=4,'y'=4,'zh'=2,'c'=2] {'zl','zh'}, dimensions={0} | all-to-all | bytes 393216 | tf_op jit(solution)/shard_map/all_to_all | solution.py:350
  181.2 1.0 shard_map.32
  (1 shorter events, 0.0 us)
Async XLA Ops:
  0.0 2.2 %copy-start = (f32[1024,8,128]{2,1,0:T(8,128)S(1)}, f32[1024,8,128]{2,1,0:T(8,128)}, u32[]{:S(2)}) copy-start(f32[1024,8,128]{2,1,0:T(8,128)} %param.1) | copy-start | bytes 12582916
  5.0 3.1 %collective-permute-start = (f32[256,128]{1,0:T(8,128)S(1)}, f32[256,128]{1,0:T(8,128)S(1)}, u32[]{:S(2)}, u32[]{:S(2)}) collective-permute-start(f32[256,128]{1,0:T(8,128)S(1)} %get-tuple-element.33), channel_id=1, source_target_pairs={{0,1},{1,2},{2,3},{3,4},{4,5},{5,6},{6,7},{7,8},{8,9},{9,10},{10,1... | collective-permute-start | bytes 393224 | tf_op jit(solution)/shard_map/ppermute | solution.py:269
  6.8 9.3 %collective-permute-start.1 = (f32[256,128]{1,0:T(8,128)S(1)}, f32[256,128]{1,0:T(8,128)S(1)}, u32[]{:S(2)}, u32[]{:S(2)}) collective-permute-start(f32[256,128]{1,0:T(8,128)S(1)} %get-tuple-element.34.order_ref.refs_0_), channel_id=1, source_target_pairs={{1,0},{2,1},{3,2},{4,3},{5,4},{6,5},{7,6},{8,7},{9,8},{10,9},{11,1... | collective-permute-start | bytes 393224 | tf_op jit(solution)/shard_map/ppermute | solution.py:269
  20.2 26.1 %collective-permute-start.2 = (f32[4,256,128]{2,1,0:T(8,128)S(1)}, f32[4,256,128]{2,1,0:T(8,128)S(1)}, u32[]{:S(2)}, u32[]{:S(2)}) collective-permute-start(f32[4,256,128]{2,1,0:T(8,128)S(1)} %get-tuple-element.35.bot_ref), channel_id=1, source_target_pairs={{0,16},{16,32},{32,48},{48,64},{64,80},{80,96},{96,112},{112,128},... | collective-permute-start | bytes 1572872 | tf_op jit(solution)/shard_map/ppermute | solution.py:269
  23.1 30.0 %collective-permute-start.3 = (f32[4,256,128]{2,1,0:T(8,128)S(1)}, f32[4,256,128]{2,1,0:T(8,128)S(1)}, u32[]{:S(2)}, u32[]{:S(2)}) collective-permute-start(f32[4,256,128]{2,1,0:T(8,128)S(1)} %get-tuple-element.36.top_ref.order_ref), channel_id=1, source_target_pairs={{16,0},{32,16},{48,32},{64,48},{80,64},{96,80},{112,96},{128,112},... | collective-permute-start | bytes 1572872 | tf_op jit(solution)/shard_map/ppermute | solution.py:269
  30.2 26.6 %collective-permute-start.4 = (f32[4,256,128]{2,1,0:T(8,128)S(1)}, f32[4,256,128]{2,1,0:T(8,128)S(1)}, u32[]{:S(2)}, u32[]{:S(2)}) collective-permute-start(f32[4,256,128]{2,1,0:T(8,128)S(1)} %get-tuple-element.38.bot_ref), channel_id=1, source_target_pairs={{0,16},{16,32},{32,48},{48,64},{64,80},{80,96},{96,112},{112,128},... | collective-permute-start | bytes 1572872 | tf_op jit(solution)/shard_map/ppermute | solution.py:269
  33.1 37.8 %collective-permute-start.5 = (f32[4,256,128]{2,1,0:T(8,128)S(1)}, f32[4,256,128]{2,1,0:T(8,128)S(1)}, u32[]{:S(2)}, u32[]{:S(2)}) collective-permute-start(f32[4,256,128]{2,1,0:T(8,128)S(1)} %get-tuple-element.39.top_ref.order_ref), channel_id=1, source_target_pairs={{16,0},{32,16},{48,32},{64,48},{80,64},{96,80},{112,96},{128,112},... | collective-permute-start | bytes 1572872 | tf_op jit(solution)/shard_map/ppermute | solution.py:269
  40.2 46.6 %collective-permute-start.8 = (f32[4,256,128]{2,1,0:T(8,128)S(1)}, f32[4,256,128]{2,1,0:T(8,128)S(1)}, u32[]{:S(2)}, u32[]{:S(2)}) collective-permute-start(f32[4,256,128]{2,1,0:T(8,128)S(1)} %get-tuple-element.44.top_ref.order_ref), channel_id=1, source_target_pairs={{16,0},{32,16},{48,32},{64,48},{80,64},{96,80},{112,96},{128,112},... | collective-permute-start | bytes 1572872 | tf_op jit(solution)/shard_map/ppermute | solution.py:269
  46.3 42.6 %collective-permute-start.10 = (f32[4,256,128]{2,1,0:T(8,128)S(1)}, f32[4,256,128]{2,1,0:T(8,128)S(1)}, u32[]{:S(2)}, u32[]{:S(2)}) collective-permute-start(f32[4,256,128]{2,1,0:T(8,128)S(1)} %get-tuple-element.48.bot_ref), channel_id=1, source_target_pairs={{0,16},{16,32},{32,48},{48,64},{64,80},{80,96},{96,112},{112,128},... | collective-permute-start | bytes 1572872 | tf_op jit(solution)/shard_map/ppermute | solution.py:269
  53.1 24.0 %collective-permute-start.7 = (f32[4,256,128]{2,1,0:T(8,128)S(1)}, f32[4,256,128]{2,1,0:T(8,128)S(1)}, u32[]{:S(2)}, u32[]{:S(2)}) collective-permute-start(f32[4,256,128]{2,1,0:T(8,128)S(1)} %get-tuple-element.43.bot_ref), channel_id=1, source_target_pairs={{0,16},{16,32},{32,48},{48,64},{64,80},{80,96},{96,112},{112,128},... | collective-permute-start | bytes 1572872 | tf_op jit(solution)/shard_map/ppermute | solution.py:269
  56.8 59.1 %collective-permute-start.11 = (f32[4,256,128]{2,1,0:T(8,128)S(1)}, f32[4,256,128]{2,1,0:T(8,128)S(1)}, u32[]{:S(2)}, u32[]{:S(2)}) collective-permute-start(f32[4,256,128]{2,1,0:T(8,128)S(1)} %get-tuple-element.49.top_ref), channel_id=1, source_target_pairs={{16,0},{32,16},{48,32},{64,48},{80,64},{96,80},{112,96},{128,112},... | collective-permute-start | bytes 1572872 | tf_op jit(solution)/shard_map/ppermute | solution.py:269
  72.9 43.0 %collective-permute-start.6 = (f32[4,32,8,128]{3,2,1,0:T(8,128)S(1)}, f32[4,32,8,128]{3,2,1,0:T(8,128)S(1)}, u32[]{:S(2)}, u32[]{:S(2)}) collective-permute-start(f32[4,32,8,128]{3,2,1,0:T(8,128)S(1)} %get-tuple-element.42), channel_id=1, source_target_pairs={{0,1},{1,0},{2,3},{3,2},{4,5},{5,4},{6,7},{7,6},{8,9},{9,8},{10,11... | collective-permute-start | bytes 1572872 | tf_op jit(solution)/shard_map/ppermute | solution.py:331
  118.2 4.9 %collective-permute-start.12 = (f32[4,59,8,128]{3,2,1,0:T(8,128)S(1)}, f32[4,59,8,128]{3,2,1,0:T(8,128)S(1)}, u32[]{:S(2)}, u32[]{:S(2)}) collective-permute-start(f32[4,59,8,128]{3,2,1,0:T(8,128)S(1)} %get-tuple-element.60), channel_id=1, source_target_pairs={{0,1},{1,0},{2,3},{3,2},{4,5},{5,4},{6,7},{7,6},{8,9},{9,8},{10,11... | collective-permute-start | bytes 2899976 | tf_op jit(solution)/shard_map/ppermute | solution.py:331
  120.1 3.1 %collective-permute-start.9 = (f32[4,40,8,128]{3,2,1,0:T(8,128)S(1)}, f32[4,40,8,128]{3,2,1,0:T(8,128)S(1)}, u32[]{:S(2)}, u32[]{:S(2)}) collective-permute-start(f32[4,40,8,128]{3,2,1,0:T(8,128)S(1)} %get-tuple-element.47), channel_id=1, source_target_pairs={{0,1},{1,0},{2,3},{3,2},{4,5},{5,4},{6,7},{7,6},{8,9},{9,8},{10,11... | collective-permute-start | bytes 1966088 | tf_op jit(solution)/shard_map/ppermute | solution.py:331
where the time goes:
time: 183 us; the launch traced here: 182 us
  waiting for transfers between devices  61.4 us (34%)
  blocking collectives  55.8 us (30%)
  starting transfers between devices  32.6 us (18%)
  Pallas kernels  30 us (16%)
  local copies, waits for them, and re-layouts  2.19 us (1%)
    ppermute x10, waiting for transfers between devices, swap(): return (lax.ppermute(ahead, axes, up), lax.ppermute(back, axes, down))  58.4 us
    all_to_all x1, blocking collectives, local(): part = lax.all_to_all(part, ('x', 'y'), 0, 0, tiled=True)  40.6 us
    ppermute x10, starting transfers between devices, swap(): return (lax.ppermute(ahead, axes, up), lax.ppermute(back, axes, down))  26.5 us
    pallas_call x4, Pallas kernels, smooth_rows(): pl.pallas_call(functools.partial(row_pass, group, count), in_specs=[vmem]...  16.5 us
    all_to_all x1, blocking collectives, local(): part = lax.all_to_all(part, ('zl', 'zh'), 0, 0, tiled=True)  15.2 us
    ppermute x3, starting transfers between devices, local(): parts += [keep, lax.ppermute(send, 'c', [(0, 1), (1, 0)])]  6.09 us
    pallas_call x4, Pallas kernels, local(): pl.pallas_call(column_pass, in_specs=[vmem] * 4 + [anywhere] * len(order)...  4.62 us
  transfers between devices with their start and end apart: 13, of which 6 were waited for; matrix products, arithmetic and copies ran while one was open for 0% of the time, Pallas kernels for 10%

commit v1 on v0

--- a/solution.py
+++ b/solution.py
@@ -74,13 +74,14 @@
     return jnp.dot(wide, w, precision=HI, preferred_element_type=f32)
 
 
-def row_pass(group, count, x_ref, left_ref, right_ref, w_ref, order_ref, top_ref, bot_ref):
-    for part in range(2 * count):
+def row_pass(start, count, x_ref, left_ref, right_ref, w_ref, order_ref, top_ref, bot_ref):
+    for part in range(count):
         at = slice(part * 128, (part + 1) * 128)
-        edge = slice(part % 2 * 128, part % 2 * 128 + 128)
-        halo = halo_lanes(group + part // 2, left_ref[edge], right_ref[edge])
+        group, half = divmod(start + part, 2)
+        edge = slice(half * 128, half * 128 + 128)
+        halo = halo_lanes(group, left_ref[edge], right_ref[edge])
         for r in range(8):
-            smooth = smooth_row(x_ref[2 * group + part, pl.ds(r, 128, stride=8), :], halo, w_ref[r])
+            smooth = smooth_row(x_ref[part, pl.ds(r, 128, stride=8), :], halo, w_ref[r])
             if r < 4:
                 top_ref[r, at] = smooth
             else:
@@ -126,10 +127,11 @@
     spread_ref[...], mean_ref[...] = to_lanes(square_ref[...], level_ref[...])
 
 
-def gram(blocks, *refs):
+def gram(blocks, pieces, *refs):
     count = 1 + max(a for a, b in blocks)
     units, refs = refs[:count], refs[count:]
-    vectors, (keep_ref, send_ref) = refs[:-2], refs[-2:]
+    vectors, keep_ref, sends = refs[:-1 - pieces], refs[-1 - pieces], refs[-pieces:]
+    each = len(blocks) * 8 // pieces if pieces > 1 else sends[0].shape[1]
     first = lax.axis_index("c") == 0
     sub = lax.broadcasted_iota(jnp.int32, (8, 128), 0)
     for n, (row, col) in enumerate(blocks):
@@ -143,31 +145,50 @@
                     c0 = jnp.where(sub < 4, a, pltpu.roll(b, 4, 0))
                     c1 = jnp.where(sub < 4, pltpu.roll(a, 4, 0), b)
                     keep_ref[y, n * 8 + zl * 2 + cb] = jnp.where(first, c0, c1)
-                    send_ref[y, n * 8 + zl * 2 + cb] = jnp.where(first, c1, c0)
+                    tile = n * 8 + zl * 2 + cb
+                    sends[tile // each][y, tile % each] = jnp.where(first, c1, c0)
     if vectors:
-        spread_ref, mean_ref = vectors
+        spread_ref, mean_ref = vectors[:2]
         end = len(blocks) * 8
         for y in range(4):
-            for ref, own, other in ((keep_ref, 1, 2), (send_ref, 2, 1)):
+            for ref, own, other in ((keep_ref, 1, 2), (sends[0], 2, 1)):
                 ref[y, end] = spread_ref[...]
                 ref[y, end + own] = mean_ref[...]
                 ref[y, end + other] = jnp.zeros((8, 128), f32)
 
 
-def merge(*refs):
-    parts, out_ref = refs[:-1], refs[-1]
+def by_turn(early_ref, early_other_ref, late_ref, *refs):
+    others, outs = refs[:-4], refs[-4:]
+    y = lax.axis_index("y")
+    start = early_ref.shape[1]
+    each = late_ref.shape[1] // len(others)
+    for turn, ref in enumerate(outs):
+        to = (y + turn) % 4
+        ref[:start] = early_ref[to] + early_other_ref[to]
+        for n, other in enumerate(others):
+            ref[start + n * each:start + (n + 1) * each] = late_ref[to, n * each:(n + 1) * each] + other[to]
+
+
+def add(*refs):
+    refs[-1][...] = refs[0][...] + refs[1][...]
+
+
+def regroup(*refs):
+    last, out_ref = refs[-2:]
     for q, blocks in enumerate(PARTS):
-        keep, other = parts[2 * q:2 * q + 2]
+        turns = refs[0:4] if q < 2 else [last.at[y] for y in range(4)]
+        start = len(PARTS[0]) * 8 if q == 1 else 0
         for n, (row, col) in enumerate(blocks):
-            for y in range(4):
-                for zl in range(4):
-                    at, to = n * 8 + zl * 2, zl * 8 + col * 2
-                    out_ref[row * 4 + y, to:to + 2] = keep[y, at:at + 2] + other[y, at:at + 2]
-    keep, other = parts[-2:]
+            for zl in range(4):
+                at, to = start + n * 8 + zl * 2, zl * 8 + col * 2
+                a, b, c, d = [ref[at:at + 2] for ref in turns]
+                out_ref[row, to:to + 2] = (a + b) + (c + d)
     end = len(PARTS[-1]) * 8
+    spread = (last[0, end] + last[1, end]) + (last[2, end] + last[3, end])
     for x in range(4):
+        out_ref[x, 32] = spread
         for y in range(4):
-            out_ref[x * 4 + y, 32:35] = keep[y, end:end + 3] + other[y, end:end + 3]
+            out_ref[x, 33 + 2 * y:35 + 2 * y] = last[y, end + 1:end + 3]
 
 
 def between(shift_ref, select):
@@ -186,19 +207,19 @@
     lane = lax.broadcasted_iota(jnp.int32, (8, 128), 1)
 
     def summed(t):
-        s = part_ref[0, t]
-        for p in range(1, 16):
-            s = s + part_ref[p, t]
-        return s
-
-    mean = (summed(33) + summed(34)) * f32(1.0 / 32)
+        return (part_ref[0, t] + part_ref[1, t]) + (part_ref[2, t] + part_ref[3, t])
+
+    mean = summed(33)
+    for k in range(1, 8):
+        mean = mean + summed(33 + k)
+    mean = mean * f32(1.0 / 32)
     spread = summed(32)
-    for k in range(2):
-        for p in range(16):
+    for k in range(8):
+        for p in range(4):
             shift = part_ref[p, 33 + k] - mean
             spread = spread + shift * shift * f32(TILE)
             for cb in range(8):
-                shift_ref[cb, k * 16 + p:k * 16 + p + 1, :] = shift[cb:cb + 1]
+                shift_ref[cb, k * 4 + p:k * 4 + p + 1, :] = shift[cb:cb + 1]
     select = []
     for zl in range(4):
         want = (zl % 2) * 64 + y * 16 + (sub // 4) * 8 + c * 4 + sub % 4
@@ -274,7 +295,7 @@
         in_specs=[pl.BlockSpec((4, 512, 128), lambda i: (0, i, 0))],
         out_specs=[pl.BlockSpec((64, 128), lambda i: (i, 0))] * 2,
         out_shape=edge_shape,
-        compiler_params=params,
+        compiler_params=pltpu.CompilerParams(vmem_limit_bytes=60 * 1024 * 1024),
     )(by_group)
     edges = swap(GY, right, left)
     weights = pl.pallas_call(
@@ -285,60 +306,77 @@
         compiler_params=params,
     )(left)
 
-    def smooth_rows(group, count, order):
+    def smooth_rows(start, count, order):
         top, bot = pl.pallas_call(
-            functools.partial(row_pass, group, count),
-            in_specs=[vmem] * 4 + [anywhere],
+            functools.partial(row_pass, start, count),
+            grid=(1,),
+            in_specs=[pl.BlockSpec((count, 1024, 128), lambda i: (start // count, 0, 0))] + [vmem] * 3 + [anywhere],
             out_specs=[vmem] * 2,
-            out_shape=[shape((4, 256 * count, 128), f32)] * 2,
+            out_shape=[shape((4, 128 * count, 128), f32)] * 2,
             compiler_params=params,
         )(by_eighth, *edges, weights, order)
         above, below = swap(GX, bot, top)
         return above, top, bot, below
 
-    chunks = []
-    for group, count in [(0, 1), (1, 1), (2, 1), (3, 1)]:
-        chunks.append(smooth_rows(group, count, chunks[-1][1] if chunks else left))
-    units, spreads, means, parts = [], [], [], []
-    order = [left]
-    for q, sources in enumerate(chunks):
-        unit, spread, mean = pl.pallas_call(
+    def columns(sources, order):
+        count = sources[0].shape[1]
+        return pl.pallas_call(
             column_pass,
             in_specs=[vmem] * 4 + [anywhere] * len(order),
             out_specs=[vmem] * 3,
-            out_shape=unit_shape(256),
-            scratch_shapes=[pltpu.VMEM((256, 128), f32)] * 2,
+            out_shape=unit_shape(count),
+            scratch_shapes=[pltpu.VMEM((count, 128), f32)] * 2,
             compiler_params=params,
         )(*sources, *order)
-        units.append(unit)
-        spreads.append(spread)
-        means.append(mean)
-        order = [unit]
-        if q == 0:
-            continue
-        blocks = PARTS[q - 1]
-        vectors = []
-        if q == 3:
-            vectors = [jnp.concatenate(v, axis=1).reshape(8, 128) for v in (spreads, means)]
-        tiles = len(blocks) * 8 + (3 if vectors else 0)
-        keep, send = pl.pallas_call(
-            functools.partial(gram, blocks),
-            in_specs=[vmem] * (len(units) + len(vectors)),
-            out_specs=[vmem] * 2,
-            out_shape=[shape((4, tiles, 8, 128), f32)] * 2,
+
+    def multiply(blocks, pieces, *operands):
+        tiles = len(blocks) * 8 + (3 if len(operands) > 4 else 0)
+        keep, *send = pl.pallas_call(
+            functools.partial(gram, blocks, pieces),
+            in_specs=([vmem] * 6 + [anywhere] * 4)[:len(operands)],
+            out_specs=[vmem] * (1 + pieces),
+            out_shape=[shape((4, tiles, 8, 128), f32)] + [shape((4, tiles // pieces, 8, 128), f32)] * pieces,
             compiler_params=params,
-        )(*units, *vectors)
-        parts += [keep, lax.ppermute(send, "c", [(0, 1), (1, 0)])]
-        order = [keep, parts[1]] if q == 2 else [keep]
+        )(*operands)
+        return [keep] + [lax.ppermute(piece, "c", [(0, 1), (1, 0)]) for piece in send]
+
+    chunks = []
+    for start in (0, 2, 4, 6):
+        chunks.append(smooth_rows(start, 2, chunks[-1][1] if chunks else left))
+    results = [columns(chunks[0], [chunks[3][1]])]
+    results.append(columns(chunks[1], [results[0][0]]))
+    early = multiply(PARTS[0], 1, *[result[0] for result in results])
+    results.append(columns(chunks[2], [early[0]]))
+    late = multiply(PARTS[1], 8, *[result[0] for result in results])
+    turns = pl.pallas_call(
+        by_turn,
+        in_specs=[vmem] * (3 + 8),
+        out_specs=[vmem] * 4,
+        out_shape=[shape((72, 8, 128), f32)] * 4,
+        compiler_params=params,
+    )(*early, *late)
+    moved = [lax.ppermute(turns[k], "y", [(i, (i + k) % 4) for i in range(4)]) for k in range(1, 4)]
+    results.append(columns(chunks[3], [turns[0]]))
+    units, spreads, means = zip(*results)
+    vectors = [jnp.concatenate(v, axis=1).reshape(8, 128) for v in (spreads, means)]
+    keep, other = multiply(PARTS[2], 1, *units, *vectors, *moved)
+    last = pl.pallas_call(
+        add,
+        in_specs=[vmem] * 2,
+        out_specs=vmem,
+        out_shape=shape(keep.shape, f32),
+        compiler_params=params,
+    )(keep, other)
+    parts = [turns[0]] + moved + [lax.all_to_all(last, "y", 0, 0, tiled=True)]
 
     part = pl.pallas_call(
-        merge,
-        in_specs=[vmem] * 6,
+        regroup,
+        in_specs=[vmem] * 5,
         out_specs=vmem,
-        out_shape=shape((16, 35, 8, 128), f32),
+        out_shape=shape((4, 41, 8, 128), f32),
         compiler_params=params,
     )(*parts)
-    part = lax.all_to_all(part, ("x", "y"), 0, 0, tiled=True)
+    part = lax.all_to_all(part, "x", 0, 0, tiled=True)
     part = pl.pallas_call(
         fold,
         in_specs=[vmem],

time: 183 us -> 182 us (level)
  starting transfers between devices: 32.6 us -> 75.6 us
  waiting for transfers between devices: 61.4 us -> 23.9 us
  Pallas kernels: 30 us -> 27 us
  blocking collectives: 55.8 us -> 53.4 us
    ppermute x10, waiting for transfers between devices: 58.4 us -> 6.74 us  [swap(): return (lax.ppermute(ahead, axes, up), lax.ppermute(back, axes, down))]
    ppermute x3 -> x13, starting transfers between devices: 6.09 us -> 45.3 us  [the longest x10 31.2 us: multiply(): lax.ppermute(piece, 'c', [(0, 1), (1, 0)])]
    ppermute x3 -> x13, waiting for transfers between devices: 3.01 us -> 17.2 us  [the longest x3 11.2 us: local(): lax.ppermute(turns[k], 'y', [(i, (i + k) % 4) for i in range(4)])]
    pallas_call x12 -> x14, Pallas kernels: 25.6 us -> 20.4 us  [the longest x4 12.6 us: smooth_rows(): pl.pallas_call(functools.partial(row_pass, start, count), grid=(1,), in_s...]
    ppermute x10, starting transfers between devices: 26.5 us -> 30.4 us  [swap(): return (lax.ppermute(ahead, axes, up), lax.ppermute(back, axes, down))]
    pallas_call x1, Pallas kernels: 2.81 us -> 5.06 us  [local(): pl.pallas_call(survey, grid=(4,), in_specs=[pl.BlockSpec((4, 512, 128), l...]
    all_to_all x1 -> x2, blocking collectives: 40.6 us -> 39.8 us  [the longest x1 21.9 us: local(): part = lax.all_to_all(part, 'x', 0, 0, tiled=True)]
  transfers between devices with their start and end apart: 13 -> 23, of which waited for: 6 -> 10; matrix products, arithmetic and copies ran while one was open for 0% -> 0% of each run, Pallas kernels for 10% -> 9%
where the time goes in v1:
time: 182 us; the launch traced here: 181 us
  starting transfers between devices  75.6 us (42%)
  blocking collectives  53.4 us (29%)
  Pallas kernels  27 us (15%)
  waiting for transfers between devices  23.9 us (13%)
    ppermute x10, starting transfers between devices, multiply(): lax.ppermute(piece, 'c', [(0, 1), (1, 0)])  31.2 us
    ppermute x10, starting transfers between devices, swap(): return (lax.ppermute(ahead, axes, up), lax.ppermute(back, axes, down))  30.4 us
    all_to_all x1, blocking collectives, local(): part = lax.all_to_all(part, 'x', 0, 0, tiled=True)  21.9 us
    all_to_all x1, blocking collectives, local(): parts = [turns[0]] + moved + [lax.all_to_all(last, 'y', 0, 0, tiled=True)]  18 us
    ppermute x3, starting transfers between devices, local(): lax.ppermute(turns[k], 'y', [(i, (i + k) % 4) for i in range(4)])  14.1 us
    all_to_all x1, blocking collectives, local(): part = lax.all_to_all(part, ('zl', 'zh'), 0, 0, tiled=True)  13.6 us
    pallas_call x4, Pallas kernels, smooth_rows(): pl.pallas_call(functools.partial(row_pass, start, count), grid=(1,), in_s...  12.6 us
    ppermute x3, waiting for transfers between devices, local(): lax.ppermute(turns[k], 'y', [(i, (i + k) % 4) for i in range(4)])  11.2 us
  transfers between devices with their start and end apart: 23, of which 10 were waited for; matrix products, arithmetic and copies ran while one was open for 0% of the time, Pallas kernels for 9%

profile of v1, /device:TPU:32, one launch (start us, length us, event | category | flops | bytes accessed | tf_op | source)
XLA Modules:
  0.0 181.1 jit_solution(5970940070454288648)
XLA Ops:
  0.0 5.1 %shard_map.17 = (f32[256,128]{1,0:T(8,128)}, f32[256,128]{1,0:T(8,128)}) custom-call(f32[4,2048,128]{2,1,0:T(8,128)} %bitcast.6), custom_call_target="tpu_custom_call" | custom-call | tf_op jit(solution)/shard_map/pallas_call | solution.py:292
  5.1 1.3 collective-permute-start.1
  6.3 3.0 %collective-permute-start = (f32[256,128]{1,0:T(8,128)}, f32[256,128]{1,0:T(8,128)S(1)}, u32[]{:S(2)}, u32[]{:S(2)}) collective-permute-start(f32[256,128]{1,0:T(8,128)} %get-tuple-element.44), channel_id=1, source_target_pairs={{0,1},{1,2},{2,3},{3,4},{4,5},{5,6},{6,7},{7,8},{8,9},{9,10},{10,1... | collective-permute-start | bytes 393224 | tf_op jit(solution)/shard_map/ppermute | solution.py:290
  9.4 0.9 copy-done
  10.4 0.2 collective-permute-done.left_ref
  10.6 3.2 %shard_map.19 = (f32[4,256,128]{2,1,0:T(8,128)S(1)}, f32[4,256,128]{2,1,0:T(8,128)S(1)}) custom-call(f32[8,1024,128]{2,1,0:T(8,128)} %bitcast.7, f32[256,128]{1,0:T(8,128)S(1)} %collective-permute-done.left_ref, f32[256,128]{1,0:T(8,128)S(1)} %collective-permute-done.1.right_ref, f32[8,256,128]{2,1,0:T(8,128)S(1)} %shard_map.18.w_ref, f32[256,128]{1,0:T(8,128)S(1)} %copy-done), custom_call_target="tpu_custom_call" | custom-call | tf_op jit(solution)/shard_map/pallas_call | solution.py:310
  13.7 3.8 %collective-permute-start.3 = (f32[4,256,128]{2,1,0:T(8,128)S(1)}, f32[4,256,128]{2,1,0:T(8,128)S(1)}, u32[]{:S(2)}, u32[]{:S(2)}) collective-permute-start(f32[4,256,128]{2,1,0:T(8,128)S(1)} %get-tuple-element.47.order_ref.top_ref), channel_id=1, source_target_pairs={{16,0},{32,16},{48,32},{64,48},{80,64},{96,80},{112,96},{128,112},... | collective-permute-start | bytes 1572872 | tf_op jit(solution)/shard_map/ppermute | solution.py:290
  17.5 2.1 %collective-permute-start.2 = (f32[4,256,128]{2,1,0:T(8,128)S(1)}, f32[4,256,128]{2,1,0:T(8,128)S(1)}, u32[]{:S(2)}, u32[]{:S(2)}) collective-permute-start(f32[4,256,128]{2,1,0:T(8,128)S(1)} %get-tuple-element.46.bot_ref), channel_id=1, source_target_pairs={{0,16},{16,32},{32,48},{48,64},{64,80},{80,96},{96,112},{112,128},... | collective-permute-start | bytes 1572872 | tf_op jit(solution)/shard_map/ppermute | solution.py:290
  19.6 3.1 %shard_map.20 = (f32[4,256,128]{2,1,0:T(8,128)S(1)}, f32[4,256,128]{2,1,0:T(8,128)S(1)}) custom-call(f32[8,1024,128]{2,1,0:T(8,128)} %bitcast.8, f32[256,128]{1,0:T(8,128)S(1)} %collective-permute-done.left_ref, f32[256,128]{1,0:T(8,128)S(1)} %collective-permute-done.1.right_ref, f32[8,256,128]{2,1,0:T(8,128)S(1)} %shard_map.18.w_ref, ...), custom_call_target="tpu_custom_call" | custom-call | tf_op jit(solution)/shard_map/pallas_call | solution.py:310
  22.7 3.8 %collective-permute-start.5 = (f32[4,256,128]{2,1,0:T(8,128)S(1)}, f32[4,256,128]{2,1,0:T(8,128)S(1)}, u32[]{:S(2)}, u32[]{:S(2)}) collective-permute-start(f32[4,256,128]{2,1,0:T(8,128)S(1)} %get-tuple-element.48.order_ref.top_ref), channel_id=1, source_target_pairs={{16,0},{32,16},{48,32},{64,48},{80,64},{96,80},{112,96},{128,112},... | collective-permute-start | bytes 1572872 | tf_op jit(solution)/shard_map/ppermute | solution.py:290
  26.5 2.1 %collective-permute-start.4 = (f32[4,256,128]{2,1,0:T(8,128)S(1)}, f32[4,256,128]{2,1,0:T(8,128)S(1)}, u32[]{:S(2)}, u32[]{:S(2)}) collective-permute-start(f32[4,256,128]{2,1,0:T(8,128)S(1)} %get-tuple-element.52.bot_ref), channel_id=1, source_target_pairs={{0,16},{16,32},{32,48},{48,64},{64,80},{80,96},{96,112},{112,128},... | collective-permute-start | bytes 1572872 | tf_op jit(solution)/shard_map/ppermute | solution.py:290
  28.6 3.1 %shard_map.21 = (f32[4,256,128]{2,1,0:T(8,128)S(1)}, f32[4,256,128]{2,1,0:T(8,128)S(1)}) custom-call(f32[8,1024,128]{2,1,0:T(8,128)} %bitcast.9, f32[256,128]{1,0:T(8,128)S(1)} %collective-permute-done.left_ref, f32[256,128]{1,0:T(8,128)S(1)} %collective-permute-done.1.right_ref, f32[8,256,128]{2,1,0:T(8,128)S(1)} %shard_map.18.w_ref, ...), custom_call_target="tpu_custom_call" | custom-call | tf_op jit(solution)/shard_map/pallas_call | solution.py:310
  31.7 3.8 %collective-permute-start.8 = (f32[4,256,128]{2,1,0:T(8,128)S(1)}, f32[4,256,128]{2,1,0:T(8,128)S(1)}, u32[]{:S(2)}, u32[]{:S(2)}) collective-permute-start(f32[4,256,128]{2,1,0:T(8,128)S(1)} %get-tuple-element.49.order_ref.top_ref), channel_id=1, source_target_pairs={{16,0},{32,16},{48,32},{64,48},{80,64},{96,80},{112,96},{128,112},... | collective-permute-start | bytes 1572872 | tf_op jit(solution)/shard_map/ppermute | solution.py:290
  35.6 4.5 %collective-permute-start.7 = (f32[4,256,128]{2,1,0:T(8,128)S(1)}, f32[4,256,128]{2,1,0:T(8,128)S(1)}, u32[]{:S(2)}, u32[]{:S(2)}) collective-permute-start(f32[4,256,128]{2,1,0:T(8,128)S(1)} %get-tuple-element.56.bot_ref), channel_id=1, source_target_pairs={{0,16},{16,32},{32,48},{48,64},{64,80},{80,96},{96,112},{112,128},... | collective-permute-start | bytes 1572872 | tf_op jit(solution)/shard_map/ppermute | solution.py:290
  40.1 3.2 %shard_map.22 = (f32[4,256,128]{2,1,0:T(8,128)S(1)}, f32[4,256,128]{2,1,0:T(8,128)S(1)}) custom-call(f32[8,1024,128]{2,1,0:T(8,128)} %bitcast.10, f32[256,128]{1,0:T(8,128)S(1)} %collective-permute-done.left_ref, f32[256,128]{1,0:T(8,128)S(1)} %collective-permute-done.1.right_ref, f32[8,256,128]{2,1,0:T(8,128)S(1)} %shard_map.18.w_ref, ...), custom_call_target="tpu_custom_call" | custom-call | tf_op jit(solution)/shard_map/pallas_call | solution.py:310
  43.3 1.2 shard_map.23
  44.4 6.5 %collective-permute-done.5.below_ref = f32[4,256,128]{2,1,0:T(8,128)S(1)} collective-permute-done((f32[4,256,128]{2,1,0:T(8,128)S(1)}, f32[4,256,128]{2,1,0:T(8,128)S(1)}, u32[]{:S(2)}, u32[]{:S(2)}) %collective-permute-start.5) | collective-permute-done | bytes 524320 | tf_op jit(solution)/shard_map/ppermute | solution.py:290
  51.0 1.2 shard_map.24
  52.2 0.8 shard_map.25
  52.9 18.9 %collective-permute-start.6 = (f32[4,32,8,128]{3,2,1,0:T(8,128)S(1)}, f32[4,32,8,128]{3,2,1,0:T(8,128)S(1)}, u32[]{:S(2)}, u32[]{:S(2)}) collective-permute-start(f32[4,32,8,128]{3,2,1,0:T(8,128)S(1)} %get-tuple-element.55), channel_id=1, source_target_pairs={{0,1},{1,0},{2,3},{3,2},{4,5},{5,4},{6,7},{7,6},{8,9},{9,8},{10,11... | collective-permute-start | bytes 1572872 | tf_op jit(solution)/shard_map/ppermute | solution.py:341
  71.8 1.9 %collective-permute-start.21 = (f32[4,256,128]{2,1,0:T(8,128)S(1)}, f32[4,256,128]{2,1,0:T(8,128)S(1)}, u32[]{:S(2)}, u32[]{:S(2)}) collective-permute-start(f32[4,256,128]{2,1,0:T(8,128)S(1)} %get-tuple-element.50.refs_0_.top_ref), channel_id=1, source_target_pairs={{16,0},{32,16},{48,32},{64,48},{80,64},{96,80},{112,96},{128,112},... | collective-permute-start | bytes 1572872 | tf_op jit(solution)/shard_map/ppermute | solution.py:290
  73.7 4.1 %collective-permute-start.20 = (f32[4,256,128]{2,1,0:T(8,128)S(1)}, f32[4,256,128]{2,1,0:T(8,128)S(1)}, u32[]{:S(2)}, u32[]{:S(2)}) collective-permute-start(f32[4,256,128]{2,1,0:T(8,128)S(1)} %get-tuple-element.71.bot_ref), channel_id=1, source_target_pairs={{0,16},{16,32},{32,48},{48,64},{64,80},{80,96},{96,112},{112,128},... | collective-permute-start | bytes 1572872 | tf_op jit(solution)/shard_map/ppermute | solution.py:290
  77.9 1.2 shard_map.26
  79.0 0.9 shard_map.27
  79.9 10.6 %collective-permute-start.10 = (f32[4,5,8,128]{3,2,1,0:T(8,128)S(1)}, f32[4,5,8,128]{3,2,1,0:T(8,128)S(1)}, u32[]{:S(2)}, u32[]{:S(2)}) collective-permute-start(f32[4,5,8,128]{3,2,1,0:T(8,128)S(1)} %get-tuple-element.60), channel_id=1, source_target_pairs={{0,1},{1,0},{2,3},{3,2},{4,5},{5,4},{6,7},{7,6},{8,9},{9,8},{10,11... | collective-permute-start | bytes 245768 | tf_op jit(solution)/shard_map/ppermute | solution.py:341
  90.6 0.8 collective-permute-done.10.refs_1_
  91.4 0.4 collective-permute-start.12
  91.8 0.2 collective-permute-start.13
  91.9 0.8 collective-permute-done.12.refs_3_
  92.7 0.4 collective-permute-start.14
  93.1 0.2 collective-permute-start.15
  93.2 0.8 collective-permute-done.14.refs_5_
  94.0 0.4 collective-permute-start.16
  94.5 0.8 collective-permute-done.16.refs_7_
  95.3 0.4 collective-permute-done.9.refs_0_
  95.8 9.7 %collective-permute-start.17 = (f32[72,8,128]{2,1,0:T(8,128)S(1)}, f32[72,8,128]{2,1,0:T(8,128)S(1)}, u32[]{:S(2)}, u32[]{:S(2)}) collective-permute-start(f32[72,8,128]{2,1,0:T(8,128)S(1)} %get-tuple-element.68), channel_id=1, source_target_pairs={{0,4},{4,8},{8,12},{12,0},{1,5},{5,9},{9,13},{13,1},{2,6},{6,10},{... | collective-permute-start | bytes 884744 | tf_op jit(solution)/shard_map/ppermute | solution.py:358
  105.5 3.2 %collective-permute-start.18 = (f32[72,8,128]{2,1,0:T(8,128)S(1)}, f32[72,8,128]{2,1,0:T(8,128)S(1)}, u32[]{:S(2)}, u32[]{:S(2)}) collective-permute-start(f32[72,8,128]{2,1,0:T(8,128)S(1)} %get-tuple-element.69), channel_id=1, source_target_pairs={{0,8},{4,12},{8,0},{12,4},{1,9},{5,13},{9,1},{13,5},{2,10},{6,14},... | collective-permute-start | bytes 884744 | tf_op jit(solution)/shard_map/ppermute | solution.py:358
  108.6 1.2 collective-permute-start.19
  109.8 1.2 shard_map.29
  111.0 3.7 %collective-permute-done.17.refs_6_.refs_1_ = f32[72,8,128]{2,1,0:T(8,128)S(1)} collective-permute-done((f32[72,8,128]{2,1,0:T(8,128)S(1)}, f32[72,8,128]{2,1,0:T(8,128)S(1)}, u32[]{:S(2)}, u32[]{:S(2)}) %collective-permute-start.17) | collective-permute-done | bytes 294944 | tf_op jit(solution)/shard_map/ppermute | solution.py:358
  114.7 7.5 %collective-permute-done.18.refs_7_.refs_2_ = f32[72,8,128]{2,1,0:T(8,128)S(1)} collective-permute-done((f32[72,8,128]{2,1,0:T(8,128)S(1)}, f32[72,8,128]{2,1,0:T(8,128)S(1)}, u32[]{:S(2)}, u32[]{:S(2)}) %collective-permute-start.18) | collective-permute-done | bytes 294944 | tf_op jit(solution)/shard_map/ppermute | solution.py:358
  122.2 1.2 shard_map.30
  123.5 2.5 %collective-permute-done.22.refs_1_ = f32[4,59,8,128]{3,2,1,0:T(8,128)S(1)} collective-permute-done((f32[4,59,8,128]{3,2,1,0:T(8,128)S(1)}, f32[4,59,8,128]{3,2,1,0:T(8,128)S(1)}, u32[]{:S(2)}, u32[]{:S(2)}) %collective-permute-start.22) | collective-permute-done | bytes 966688 | tf_op jit(solution)/shard_map/ppermute | solution.py:341
  126.1 18.0 %all_to_all.15.refs_4_ = f32[4,59,8,128]{3,2,1,0:T(8,128)S(1)} all-to-all(f32[4,59,8,128]{3,2,1,0:T(8,128)S(1)} %shard_map.31), channel_id=1, replica_groups=mesh['x'=4,'zl'=4,'y'=4,'zh'=2,'c'=2] {'y'}, dimensions={0} | all-to-all | bytes 1933312 | tf_op jit(solution)/shard_map/all_to_all | solution.py:370
  144.2 21.9 %all_to_all.16.part_ref = f32[4,41,8,128]{3,2,1,0:T(8,128)S(1)} all-to-all(f32[4,41,8,128]{3,2,1,0:T(8,128)S(1)} %shard_map.32), channel_id=1, replica_groups=mesh['x'=4,'zl'=4,'y'=4,'zh'=2,'c'=2] {'x'}, dimensions={0} | all-to-all | bytes 1343488 | tf_op jit(solution)/shard_map/all_to_all | solution.py:379
  166.0 0.5 shard_map.33
  166.6 13.6 %all_to_all.17.part_ref = f32[8,6,8,128]{3,2,1,0:T(8,128)S(1)} all-to-all(f32[8,6,8,128]{3,2,1,0:T(8,128)S(1)} %shard_map.33), channel_id=1, replica_groups=mesh['x'=4,'zl'=4,'y'=4,'zh'=2,'c'=2] {'zl','zh'}, dimensions={0} | all-to-all | bytes 393216 | tf_op jit(solution)/shard_map/all_to_all | solution.py:388
  180.2 1.0 shard_map.34
  (22 shorter events, 0.8 us)
Async XLA Ops:
  5.1 5.3 %collective-permute-start.1 = (f32[256,128]{1,0:T(8,128)}, f32[256,128]{1,0:T(8,128)S(1)}, u32[]{:S(2)}, u32[]{:S(2)}) collective-permute-start(f32[256,128]{1,0:T(8,128)} %get-tuple-element.45.order_ref), channel_id=1, source_target_pairs={{1,0},{2,1},{3,2},{4,3},{5,4},{6,5},{7,6},{8,7},{9,8},{10,9},{11,1... | collective-permute-start | bytes 393224 | tf_op jit(solution)/shard_map/ppermute | solution.py:290
  6.3 4.2 %collective-permute-start = (f32[256,128]{1,0:T(8,128)}, f32[256,128]{1,0:T(8,128)S(1)}, u32[]{:S(2)}, u32[]{:S(2)}) collective-permute-start(f32[256,128]{1,0:T(8,128)} %get-tuple-element.44), channel_id=1, source_target_pairs={{0,1},{1,2},{2,3},{3,4},{4,5},{5,6},{6,7},{7,8},{8,9},{9,10},{10,1... | collective-permute-start | bytes 393224 | tf_op jit(solution)/shard_map/ppermute | solution.py:290
  9.4 0.9 copy-start
  13.7 21.8 %collective-permute-start.3 = (f32[4,256,128]{2,1,0:T(8,128)S(1)}, f32[4,256,128]{2,1,0:T(8,128)S(1)}, u32[]{:S(2)}, u32[]{:S(2)}) collective-permute-start(f32[4,256,128]{2,1,0:T(8,128)S(1)} %get-tuple-element.47.order_ref.top_ref), channel_id=1, source_target_pairs={{16,0},{32,16},{48,32},{64,48},{80,64},{96,80},{112,96},{128,112},... | collective-permute-start | bytes 1572872 | tf_op jit(solution)/shard_map/ppermute | solution.py:290
  17.5 25.8 %collective-permute-start.2 = (f32[4,256,128]{2,1,0:T(8,128)S(1)}, f32[4,256,128]{2,1,0:T(8,128)S(1)}, u32[]{:S(2)}, u32[]{:S(2)}) collective-permute-start(f32[4,256,128]{2,1,0:T(8,128)S(1)} %get-tuple-element.46.bot_ref), channel_id=1, source_target_pairs={{0,16},{16,32},{32,48},{48,64},{64,80},{80,96},{96,112},{112,128},... | collective-permute-start | bytes 1572872 | tf_op jit(solution)/shard_map/ppermute | solution.py:290
  22.7 28.3 %collective-permute-start.5 = (f32[4,256,128]{2,1,0:T(8,128)S(1)}, f32[4,256,128]{2,1,0:T(8,128)S(1)}, u32[]{:S(2)}, u32[]{:S(2)}) collective-permute-start(f32[4,256,128]{2,1,0:T(8,128)S(1)} %get-tuple-element.48.order_ref.top_ref), channel_id=1, source_target_pairs={{16,0},{32,16},{48,32},{64,48},{80,64},{96,80},{112,96},{128,112},... | collective-permute-start | bytes 1572872 | tf_op jit(solution)/shard_map/ppermute | solution.py:290
  26.5 24.5 %collective-permute-start.4 = (f32[4,256,128]{2,1,0:T(8,128)S(1)}, f32[4,256,128]{2,1,0:T(8,128)S(1)}, u32[]{:S(2)}, u32[]{:S(2)}) collective-permute-start(f32[4,256,128]{2,1,0:T(8,128)S(1)} %get-tuple-element.52.bot_ref), channel_id=1, source_target_pairs={{0,16},{16,32},{32,48},{48,64},{64,80},{80,96},{96,112},{112,128},... | collective-permute-start | bytes 1572872 | tf_op jit(solution)/shard_map/ppermute | solution.py:290
  31.7 46.1 %collective-permute-start.8 = (f32[4,256,128]{2,1,0:T(8,128)S(1)}, f32[4,256,128]{2,1,0:T(8,128)S(1)}, u32[]{:S(2)}, u32[]{:S(2)}) collective-permute-start(f32[4,256,128]{2,1,0:T(8,128)S(1)} %get-tuple-element.49.order_ref.top_ref), channel_id=1, source_target_pairs={{16,0},{32,16},{48,32},{64,48},{80,64},{96,80},{112,96},{128,112},... | collective-permute-start | bytes 1572872 | tf_op jit(solution)/shard_map/ppermute | solution.py:290
  35.6 42.3 %collective-permute-start.7 = (f32[4,256,128]{2,1,0:T(8,128)S(1)}, f32[4,256,128]{2,1,0:T(8,128)S(1)}, u32[]{:S(2)}, u32[]{:S(2)}) collective-permute-start(f32[4,256,128]{2,1,0:T(8,128)S(1)} %get-tuple-element.56.bot_ref), channel_id=1, source_target_pairs={{0,16},{16,32},{32,48},{48,64},{64,80},{80,96},{96,112},{112,128},... | collective-permute-start | bytes 1572872 | tf_op jit(solution)/shard_map/ppermute | solution.py:290
  52.9 42.7 %collective-permute-start.6 = (f32[4,32,8,128]{3,2,1,0:T(8,128)S(1)}, f32[4,32,8,128]{3,2,1,0:T(8,128)S(1)}, u32[]{:S(2)}, u32[]{:S(2)}) collective-permute-start(f32[4,32,8,128]{3,2,1,0:T(8,128)S(1)} %get-tuple-element.55), channel_id=1, source_target_pairs={{0,1},{1,0},{2,3},{3,2},{4,5},{5,4},{6,7},{7,6},{8,9},{9,8},{10,11... | collective-permute-start | bytes 1572872 | tf_op jit(solution)/shard_map/ppermute | solution.py:341
  71.8 38.0 %collective-permute-start.21 = (f32[4,256,128]{2,1,0:T(8,128)S(1)}, f32[4,256,128]{2,1,0:T(8,128)S(1)}, u32[]{:S(2)}, u32[]{:S(2)}) collective-permute-start(f32[4,256,128]{2,1,0:T(8,128)S(1)} %get-tuple-element.50.refs_0_.top_ref), channel_id=1, source_target_pairs={{16,0},{32,16},{48,32},{64,48},{80,64},{96,80},{112,96},{128,112},... | collective-permute-start | bytes 1572872 | tf_op jit(solution)/shard_map/ppermute | solution.py:290
  73.7 36.1 %collective-permute-start.20 = (f32[4,256,128]{2,1,0:T(8,128)S(1)}, f32[4,256,128]{2,1,0:T(8,128)S(1)}, u32[]{:S(2)}, u32[]{:S(2)}) collective-permute-start(f32[4,256,128]{2,1,0:T(8,128)S(1)} %get-tuple-element.71.bot_ref), channel_id=1, source_target_pairs={{0,16},{16,32},{32,48},{48,64},{64,80},{80,96},{96,112},{112,128},... | collective-permute-start | bytes 1572872 | tf_op jit(solution)/shard_map/ppermute | solution.py:290
  79.9 11.5 %collective-permute-start.10 = (f32[4,5,8,128]{3,2,1,0:T(8,128)S(1)}, f32[4,5,8,128]{3,2,1,0:T(8,128)S(1)}, u32[]{:S(2)}, u32[]{:S(2)}) collective-permute-start(f32[4,5,8,128]{3,2,1,0:T(8,128)S(1)} %get-tuple-element.60), channel_id=1, source_target_pairs={{0,1},{1,0},{2,3},{3,2},{4,5},{5,4},{6,7},{7,6},{8,9},{9,8},{10,11... | collective-permute-start | bytes 245768 | tf_op jit(solution)/shard_map/ppermute | solution.py:341
  90.5 1.3 collective-permute-start.11
  91.4 1.3 collective-permute-start.12
  91.8 1.3 collective-permute-start.13
  92.7 1.3 collective-permute-start.14
  93.1 1.3 collective-permute-start.15
  94.0 1.3 collective-permute-start.16
  94.3 1.3 collective-permute-start.9
  95.8 18.9 %collective-permute-start.17 = (f32[72,8,128]{2,1,0:T(8,128)S(1)}, f32[72,8,128]{2,1,0:T(8,128)S(1)}, u32[]{:S(2)}, u32[]{:S(2)}) collective-permute-start(f32[72,8,128]{2,1,0:T(8,128)S(1)} %get-tuple-element.68), channel_id=1, source_target_pairs={{0,4},{4,8},{8,12},{12,0},{1,5},{5,9},{9,13},{13,1},{2,6},{6,10},{... | collective-permute-start | bytes 884744 | tf_op jit(solution)/shard_map/ppermute | solution.py:358
  105.5 16.8 %collective-permute-start.18 = (f32[72,8,128]{2,1,0:T(8,128)S(1)}, f32[72,8,128]{2,1,0:T(8,128)S(1)}, u32[]{:S(2)}, u32[]{:S(2)}) collective-permute-start(f32[72,8,128]{2,1,0:T(8,128)S(1)} %get-tuple-element.69), channel_id=1, source_target_pairs={{0,8},{4,12},{8,0},{12,4},{1,9},{5,13},{9,1},{13,5},{2,10},{6,14},... | collective-permute-start | bytes 884744 | tf_op jit(solution)/shard_map/ppermute | solution.py:358
  108.6 13.6 %collective-permute-start.19 = (f32[72,8,128]{2,1,0:T(8,128)S(1)}, f32[72,8,128]{2,1,0:T(8,128)S(1)}, u32[]{:S(2)}, u32[]{:S(2)}) collective-permute-start(f32[72,8,128]{2,1,0:T(8,128)S(1)} %get-tuple-element.70), channel_id=1, source_target_pairs={{0,12},{4,0},{8,4},{12,8},{1,13},{5,1},{9,5},{13,9},{2,14},{6,2},{... | collective-permute-start | bytes 884744 | tf_op jit(solution)/shard_map/ppermute | solution.py:358
  123.4 2.6 %collective-permute-start.22 = (f32[4,59,8,128]{3,2,1,0:T(8,128)S(1)}, f32[4,59,8,128]{3,2,1,0:T(8,128)S(1)}, u32[]{:S(2)}, u32[]{:S(2)}) collective-permute-start(f32[4,59,8,128]{3,2,1,0:T(8,128)S(1)} %get-tuple-element.82), channel_id=1, source_target_pairs={{0,1},{1,0},{2,3},{3,2},{4,5},{5,4},{6,7},{7,6},{8,9},{9,8},{10,11... | collective-permute-start | bytes 2899976 | tf_op jit(solution)/shard_map/ppermute | solution.py:341

commit v2 on v1

--- a/solution.py
+++ b/solution.py
@@ -14,8 +14,8 @@
 TILE = 8 * 128
 PARTS = (
     ((0, 0), (0, 1), (1, 0), (1, 1)),
-    ((2, 0), (2, 1), (2, 2), (0, 2), (1, 2)),
-    ((3, 0), (3, 1), (3, 2), (3, 3), (0, 3), (1, 3), (2, 3)),
+    ((2, 0), (2, 1), (0, 2)),
+    ((3, 0), (3, 1), (3, 2), (3, 3), (0, 3), (1, 3), (2, 3), (2, 2), (1, 2)),
 )
 GX, GY = ("x", "zl"), ("y", "zh", "c")
 AXES = GX + GY
@@ -347,12 +347,12 @@
     results.append(columns(chunks[1], [results[0][0]]))
     early = multiply(PARTS[0], 1, *[result[0] for result in results])
     results.append(columns(chunks[2], [early[0]]))
-    late = multiply(PARTS[1], 8, *[result[0] for result in results])
+    late = multiply(PARTS[1], 4, *[result[0] for result in results])
     turns = pl.pallas_call(
         by_turn,
-        in_specs=[vmem] * (3 + 8),
+        in_specs=[vmem] * (3 + 4),
         out_specs=[vmem] * 4,
-        out_shape=[shape((72, 8, 128), f32)] * 4,
+        out_shape=[shape((56, 8, 128), f32)] * 4,
         compiler_params=params,
     )(*early, *late)
     moved = [lax.ppermute(turns[k], "y", [(i, (i + k) % 4) for i in range(4)]) for k in range(1, 4)]

time: 182 us -> 180 us (0.989)
  waiting for transfers between devices: 23.9 us -> 20 us
  blocking collectives: 53.4 us -> 56.2 us
    all_to_all x1, blocking collectives: 18 us -> 24.1 us  [local(): parts = [turns[0]] + moved + [lax.all_to_all(last, 'y', 0, 0, tiled=True)]]
    all_to_all x1, blocking collectives: 21.9 us -> 18.6 us  [local(): part = lax.all_to_all(part, 'x', 0, 0, tiled=True)]
    ppermute x3, waiting for transfers between devices: 11.2 us -> 8.37 us  [local(): lax.ppermute(turns[k], 'y', [(i, (i + k) % 4) for i in range(4)])]
    ppermute x10 -> x6, waiting for transfers between devices: 6.01 us -> 4.9 us  [multiply(): lax.ppermute(piece, 'c', [(0, 1), (1, 0)])]
    ppermute x10 -> x6, starting transfers between devices: 31.2 us -> 30.2 us  [multiply(): lax.ppermute(piece, 'c', [(0, 1), (1, 0)])]
  transfers between devices with their start and end apart: 23 -> 19, of which waited for: 10 -> 8; matrix products, arithmetic and copies ran while one was open for 0% -> 0% of each run, Pallas kernels for 9% -> 9%
where the time goes in v2:
time: 180 us; the launch traced here: 179 us
  starting transfers between devices  74.6 us (41%)
  blocking collectives  56.2 us (31%)
  Pallas kernels  27.1 us (15%)
  waiting for transfers between devices  20 us (11%)
    ppermute x10, starting transfers between devices, swap(): return (lax.ppermute(ahead, axes, up), lax.ppermute(back, axes, down))  30.4 us
    ppermute x6, starting transfers between devices, multiply(): lax.ppermute(piece, 'c', [(0, 1), (1, 0)])  30.2 us
    all_to_all x1, blocking collectives, local(): parts = [turns[0]] + moved + [lax.all_to_all(last, 'y', 0, 0, tiled=True)]  24.1 us
    all_to_all x1, blocking collectives, local(): part = lax.all_to_all(part, 'x', 0, 0, tiled=True)  18.6 us
    ppermute x3, starting transfers between devices, local(): lax.ppermute(turns[k], 'y', [(i, (i + k) % 4) for i in range(4)])  14.1 us
    all_to_all x1, blocking collectives, local(): part = lax.all_to_all(part, ('zl', 'zh'), 0, 0, tiled=True)  13.6 us
    pallas_call x4, Pallas kernels, smooth_rows(): pl.pallas_call(functools.partial(row_pass, start, count), grid=(1,), in_s...  12.6 us
    ppermute x3, waiting for transfers between devices, local(): lax.ppermute(turns[k], 'y', [(i, (i + k) % 4) for i in range(4)])  8.37 us
  transfers between devices with their start and end apart: 19, of which 8 were waited for; matrix products, arithmetic and copies ran while one was open for 0% of the time, Pallas kernels for 9%

profile of v2, /device:TPU:32, one launch (start us, length us, event | category | flops | bytes accessed | tf_op | source)
XLA Modules:
  0.0 179.1 jit_solution(7757587723120199298)
XLA Ops:
  0.0 5.1 %shard_map.17 = (f32[256,128]{1,0:T(8,128)}, f32[256,128]{1,0:T(8,128)}) custom-call(f32[4,2048,128]{2,1,0:T(8,128)} %bitcast.6), custom_call_target="tpu_custom_call" | custom-call | tf_op jit(solution)/shard_map/pallas_call | solution.py:292
  5.1 1.3 collective-permute-start.1
  6.3 3.0 %collective-permute-start = (f32[256,128]{1,0:T(8,128)}, f32[256,128]{1,0:T(8,128)S(1)}, u32[]{:S(2)}, u32[]{:S(2)}) collective-permute-start(f32[256,128]{1,0:T(8,128)} %get-tuple-element.40), channel_id=1, source_target_pairs={{0,1},{1,2},{2,3},{3,4},{4,5},{5,6},{6,7},{7,8},{8,9},{9,10},{10,1... | collective-permute-start | bytes 393224 | tf_op jit(solution)/shard_map/ppermute | solution.py:290
  9.4 0.9 copy-done
  10.4 0.2 collective-permute-done.left_ref
  10.6 3.2 %shard_map.19 = (f32[4,256,128]{2,1,0:T(8,128)S(1)}, f32[4,256,128]{2,1,0:T(8,128)S(1)}) custom-call(f32[8,1024,128]{2,1,0:T(8,128)} %bitcast.7, f32[256,128]{1,0:T(8,128)S(1)} %collective-permute-done.left_ref, f32[256,128]{1,0:T(8,128)S(1)} %collective-permute-done.1.right_ref, f32[8,256,128]{2,1,0:T(8,128)S(1)} %shard_map.18.w_ref, f32[256,128]{1,0:T(8,128)S(1)} %copy-done), custom_call_target="tpu_custom_call" | custom-call | tf_op jit(solution)/shard_map/pallas_call | solution.py:310
  13.7 3.8 %collective-permute-start.3 = (f32[4,256,128]{2,1,0:T(8,128)S(1)}, f32[4,256,128]{2,1,0:T(8,128)S(1)}, u32[]{:S(2)}, u32[]{:S(2)}) collective-permute-start(f32[4,256,128]{2,1,0:T(8,128)S(1)} %get-tuple-element.43.order_ref.top_ref), channel_id=1, source_target_pairs={{16,0},{32,16},{48,32},{64,48},{80,64},{96,80},{112,96},{128,112},... | collective-permute-start | bytes 1572872 | tf_op jit(solution)/shard_map/ppermute | solution.py:290
  17.5 2.1 %collective-permute-start.2 = (f32[4,256,128]{2,1,0:T(8,128)S(1)}, f32[4,256,128]{2,1,0:T(8,128)S(1)}, u32[]{:S(2)}, u32[]{:S(2)}) collective-permute-start(f32[4,256,128]{2,1,0:T(8,128)S(1)} %get-tuple-element.42.bot_ref), channel_id=1, source_target_pairs={{0,16},{16,32},{32,48},{48,64},{64,80},{80,96},{96,112},{112,128},... | collective-permute-start | bytes 1572872 | tf_op jit(solution)/shard_map/ppermute | solution.py:290
  19.6 3.1 %shard_map.20 = (f32[4,256,128]{2,1,0:T(8,128)S(1)}, f32[4,256,128]{2,1,0:T(8,128)S(1)}) custom-call(f32[8,1024,128]{2,1,0:T(8,128)} %bitcast.8, f32[256,128]{1,0:T(8,128)S(1)} %collective-permute-done.left_ref, f32[256,128]{1,0:T(8,128)S(1)} %collective-permute-done.1.right_ref, f32[8,256,128]{2,1,0:T(8,128)S(1)} %shard_map.18.w_ref, ...), custom_call_target="tpu_custom_call" | custom-call | tf_op jit(solution)/shard_map/pallas_call | solution.py:310
  22.7 3.8 %collective-permute-start.5 = (f32[4,256,128]{2,1,0:T(8,128)S(1)}, f32[4,256,128]{2,1,0:T(8,128)S(1)}, u32[]{:S(2)}, u32[]{:S(2)}) collective-permute-start(f32[4,256,128]{2,1,0:T(8,128)S(1)} %get-tuple-element.44.order_ref.top_ref), channel_id=1, source_target_pairs={{16,0},{32,16},{48,32},{64,48},{80,64},{96,80},{112,96},{128,112},... | collective-permute-start | bytes 1572872 | tf_op jit(solution)/shard_map/ppermute | solution.py:290
  26.5 2.1 %collective-permute-start.4 = (f32[4,256,128]{2,1,0:T(8,128)S(1)}, f32[4,256,128]{2,1,0:T(8,128)S(1)}, u32[]{:S(2)}, u32[]{:S(2)}) collective-permute-start(f32[4,256,128]{2,1,0:T(8,128)S(1)} %get-tuple-element.48.bot_ref), channel_id=1, source_target_pairs={{0,16},{16,32},{32,48},{48,64},{64,80},{80,96},{96,112},{112,128},... | collective-permute-start | bytes 1572872 | tf_op jit(solution)/shard_map/ppermute | solution.py:290
  28.6 3.2 %shard_map.21 = (f32[4,256,128]{2,1,0:T(8,128)S(1)}, f32[4,256,128]{2,1,0:T(8,128)S(1)}) custom-call(f32[8,1024,128]{2,1,0:T(8,128)} %bitcast.9, f32[256,128]{1,0:T(8,128)S(1)} %collective-permute-done.left_ref, f32[256,128]{1,0:T(8,128)S(1)} %collective-permute-done.1.right_ref, f32[8,256,128]{2,1,0:T(8,128)S(1)} %shard_map.18.w_ref, ...), custom_call_target="tpu_custom_call" | custom-call | tf_op jit(solution)/shard_map/pallas_call | solution.py:310
  31.7 3.8 %collective-permute-start.8 = (f32[4,256,128]{2,1,0:T(8,128)S(1)}, f32[4,256,128]{2,1,0:T(8,128)S(1)}, u32[]{:S(2)}, u32[]{:S(2)}) collective-permute-start(f32[4,256,128]{2,1,0:T(8,128)S(1)} %get-tuple-element.45.order_ref.top_ref), channel_id=1, source_target_pairs={{16,0},{32,16},{48,32},{64,48},{80,64},{96,80},{112,96},{128,112},... | collective-permute-start | bytes 1572872 | tf_op jit(solution)/shard_map/ppermute | solution.py:290
  35.6 4.5 %collective-permute-start.7 = (f32[4,256,128]{2,1,0:T(8,128)S(1)}, f32[4,256,128]{2,1,0:T(8,128)S(1)}, u32[]{:S(2)}, u32[]{:S(2)}) collective-permute-start(f32[4,256,128]{2,1,0:T(8,128)S(1)} %get-tuple-element.52.bot_ref), channel_id=1, source_target_pairs={{0,16},{16,32},{32,48},{48,64},{64,80},{80,96},{96,112},{112,128},... | collective-permute-start | bytes 1572872 | tf_op jit(solution)/shard_map/ppermute | solution.py:290
  40.1 3.2 %shard_map.22 = (f32[4,256,128]{2,1,0:T(8,128)S(1)}, f32[4,256,128]{2,1,0:T(8,128)S(1)}) custom-call(f32[8,1024,128]{2,1,0:T(8,128)} %bitcast.10, f32[256,128]{1,0:T(8,128)S(1)} %collective-permute-done.left_ref, f32[256,128]{1,0:T(8,128)S(1)} %collective-permute-done.1.right_ref, f32[8,256,128]{2,1,0:T(8,128)S(1)} %shard_map.18.w_ref, ...), custom_call_target="tpu_custom_call" | custom-call | tf_op jit(solution)/shard_map/pallas_call | solution.py:310
  43.3 1.2 shard_map.23
  44.4 6.5 %collective-permute-done.5.below_ref = f32[4,256,128]{2,1,0:T(8,128)S(1)} collective-permute-done((f32[4,256,128]{2,1,0:T(8,128)S(1)}, f32[4,256,128]{2,1,0:T(8,128)S(1)}, u32[]{:S(2)}, u32[]{:S(2)}) %collective-permute-start.5) | collective-permute-done | bytes 524320 | tf_op jit(solution)/shard_map/ppermute | solution.py:290
  51.0 1.2 shard_map.24
  52.1 0.8 shard_map.25
  52.9 18.9 %collective-permute-start.6 = (f32[4,32,8,128]{3,2,1,0:T(8,128)S(1)}, f32[4,32,8,128]{3,2,1,0:T(8,128)S(1)}, u32[]{:S(2)}, u32[]{:S(2)}) collective-permute-start(f32[4,32,8,128]{3,2,1,0:T(8,128)S(1)} %get-tuple-element.51), channel_id=1, source_target_pairs={{0,1},{1,0},{2,3},{3,2},{4,5},{5,4},{6,7},{7,6},{8,9},{9,8},{10,11... | collective-permute-start | bytes 1572872 | tf_op jit(solution)/shard_map/ppermute | solution.py:341
  71.8 1.9 %collective-permute-start.17 = (f32[4,256,128]{2,1,0:T(8,128)S(1)}, f32[4,256,128]{2,1,0:T(8,128)S(1)}, u32[]{:S(2)}, u32[]{:S(2)}) collective-permute-start(f32[4,256,128]{2,1,0:T(8,128)S(1)} %get-tuple-element.46.refs_0_.top_ref), channel_id=1, source_target_pairs={{16,0},{32,16},{48,32},{64,48},{80,64},{96,80},{112,96},{128,112},... | collective-permute-start | bytes 1572872 | tf_op jit(solution)/shard_map/ppermute | solution.py:290
  73.7 4.1 %collective-permute-start.16 = (f32[4,256,128]{2,1,0:T(8,128)S(1)}, f32[4,256,128]{2,1,0:T(8,128)S(1)}, u32[]{:S(2)}, u32[]{:S(2)}) collective-permute-start(f32[4,256,128]{2,1,0:T(8,128)S(1)} %get-tuple-element.63.bot_ref), channel_id=1, source_target_pairs={{0,16},{16,32},{32,48},{48,64},{64,80},{80,96},{96,112},{112,128},... | collective-permute-start | bytes 1572872 | tf_op jit(solution)/shard_map/ppermute | solution.py:290
  77.9 1.2 shard_map.26
  79.0 0.6 shard_map.27
  79.7 10.6 %collective-permute-start.10 = (f32[4,6,8,128]{3,2,1,0:T(8,128)S(1)}, f32[4,6,8,128]{3,2,1,0:T(8,128)S(1)}, u32[]{:S(2)}, u32[]{:S(2)}) collective-permute-start(f32[4,6,8,128]{3,2,1,0:T(8,128)S(1)} %get-tuple-element.56), channel_id=1, source_target_pairs={{0,1},{1,0},{2,3},{3,2},{4,5},{5,4},{6,7},{7,6},{8,9},{9,8},{10,11... | collective-permute-start | bytes 294920 | tf_op jit(solution)/shard_map/ppermute | solution.py:341
  90.2 0.1 collective-permute-start.11
  90.3 0.8 collective-permute-done.10.refs_1_
  91.2 0.4 collective-permute-start.12
  91.5 0.2 collective-permute-start.9
  91.7 0.8 collective-permute-done.12.refs_3_
  92.5 0.4 collective-permute-done.9.refs_0_
  92.8 0.1 shard_map.28
  93.0 9.7 %collective-permute-start.13 = (f32[56,8,128]{2,1,0:T(8,128)S(1)}, f32[56,8,128]{2,1,0:T(8,128)S(1)}, u32[]{:S(2)}, u32[]{:S(2)}) collective-permute-start(f32[56,8,128]{2,1,0:T(8,128)S(1)} %get-tuple-element.60), channel_id=1, source_target_pairs={{0,4},{4,8},{8,12},{12,0},{1,5},{5,9},{9,13},{13,1},{2,6},{6,10},{... | collective-permute-start | bytes 688136 | tf_op jit(solution)/shard_map/ppermute | solution.py:358
  102.7 3.2 %collective-permute-start.14 = (f32[56,8,128]{2,1,0:T(8,128)S(1)}, f32[56,8,128]{2,1,0:T(8,128)S(1)}, u32[]{:S(2)}, u32[]{:S(2)}) collective-permute-start(f32[56,8,128]{2,1,0:T(8,128)S(1)} %get-tuple-element.61), channel_id=1, source_target_pairs={{0,8},{4,12},{8,0},{12,4},{1,9},{5,13},{9,1},{13,5},{2,10},{6,14},... | collective-permute-start | bytes 688136 | tf_op jit(solution)/shard_map/ppermute | solution.py:358
  105.9 1.2 collective-permute-start.15
  107.0 1.2 shard_map.29
  108.2 2.3 %collective-permute-done.13.refs_6_.refs_1_ = f32[56,8,128]{2,1,0:T(8,128)S(1)} collective-permute-done((f32[56,8,128]{2,1,0:T(8,128)S(1)}, f32[56,8,128]{2,1,0:T(8,128)S(1)}, u32[]{:S(2)}, u32[]{:S(2)}) %collective-permute-start.13) | collective-permute-done | bytes 229408 | tf_op jit(solution)/shard_map/ppermute | solution.py:358
  110.5 6.1 %collective-permute-done.14.refs_7_.refs_2_ = f32[56,8,128]{2,1,0:T(8,128)S(1)} collective-permute-done((f32[56,8,128]{2,1,0:T(8,128)S(1)}, f32[56,8,128]{2,1,0:T(8,128)S(1)}, u32[]{:S(2)}, u32[]{:S(2)}) %collective-permute-start.14) | collective-permute-done | bytes 229408 | tf_op jit(solution)/shard_map/ppermute | solution.py:358
  116.6 1.4 shard_map.30
  118.0 0.1 collective-permute-start.18
  118.1 2.9 %collective-permute-done.18.refs_1_ = f32[4,75,8,128]{3,2,1,0:T(8,128)S(1)} collective-permute-done((f32[4,75,8,128]{3,2,1,0:T(8,128)S(1)}, f32[4,75,8,128]{3,2,1,0:T(8,128)S(1)}, u32[]{:S(2)}, u32[]{:S(2)}) %collective-permute-start.18) | collective-permute-done | bytes 1228832 | tf_op jit(solution)/shard_map/ppermute | solution.py:341
  121.0 0.2 shard_map.31
  121.2 24.1 %all_to_all.15.refs_4_ = f32[4,75,8,128]{3,2,1,0:T(8,128)S(1)} all-to-all(f32[4,75,8,128]{3,2,1,0:T(8,128)S(1)} %shard_map.31), channel_id=1, replica_groups=mesh['x'=4,'zl'=4,'y'=4,'zh'=2,'c'=2] {'y'}, dimensions={0} | all-to-all | bytes 2457600 | tf_op jit(solution)/shard_map/all_to_all | solution.py:370
  145.3 0.1 shard_map.32
  145.4 18.6 %all_to_all.16.part_ref = f32[4,41,8,128]{3,2,1,0:T(8,128)S(1)} all-to-all(f32[4,41,8,128]{3,2,1,0:T(8,128)S(1)} %shard_map.32), channel_id=1, replica_groups=mesh['x'=4,'zl'=4,'y'=4,'zh'=2,'c'=2] {'x'}, dimensions={0} | all-to-all | bytes 1343488 | tf_op jit(solution)/shard_map/all_to_all | solution.py:379
  164.0 0.5 shard_map.33
  164.5 13.6 %all_to_all.17.part_ref = f32[8,6,8,128]{3,2,1,0:T(8,128)S(1)} all-to-all(f32[8,6,8,128]{3,2,1,0:T(8,128)S(1)} %shard_map.33), channel_id=1, replica_groups=mesh['x'=4,'zl'=4,'y'=4,'zh'=2,'c'=2] {'zl','zh'}, dimensions={0} | all-to-all | bytes 393216 | tf_op jit(solution)/shard_map/all_to_all | solution.py:388
  178.1 1.0 shard_map.34
  (14 shorter events, 0.1 us)
Async XLA Ops:
  5.1 5.3 %collective-permute-start.1 = (f32[256,128]{1,0:T(8,128)}, f32[256,128]{1,0:T(8,128)S(1)}, u32[]{:S(2)}, u32[]{:S(2)}) collective-permute-start(f32[256,128]{1,0:T(8,128)} %get-tuple-element.41.order_ref), channel_id=1, source_target_pairs={{1,0},{2,1},{3,2},{4,3},{5,4},{6,5},{7,6},{8,7},{9,8},{10,9},{11,1... | collective-permute-start | bytes 393224 | tf_op jit(solution)/shard_map/ppermute | solution.py:290
  6.3 4.2 %collective-permute-start = (f32[256,128]{1,0:T(8,128)}, f32[256,128]{1,0:T(8,128)S(1)}, u32[]{:S(2)}, u32[]{:S(2)}) collective-permute-start(f32[256,128]{1,0:T(8,128)} %get-tuple-element.40), channel_id=1, source_target_pairs={{0,1},{1,2},{2,3},{3,4},{4,5},{5,6},{6,7},{7,8},{8,9},{9,10},{10,1... | collective-permute-start | bytes 393224 | tf_op jit(solution)/shard_map/ppermute | solution.py:290
  9.4 0.9 copy-start
  13.7 21.8 %collective-permute-start.3 = (f32[4,256,128]{2,1,0:T(8,128)S(1)}, f32[4,256,128]{2,1,0:T(8,128)S(1)}, u32[]{:S(2)}, u32[]{:S(2)}) collective-permute-start(f32[4,256,128]{2,1,0:T(8,128)S(1)} %get-tuple-element.43.order_ref.top_ref), channel_id=1, source_target_pairs={{16,0},{32,16},{48,32},{64,48},{80,64},{96,80},{112,96},{128,112},... | collective-permute-start | bytes 1572872 | tf_op jit(solution)/shard_map/ppermute | solution.py:290
  17.5 25.8 %collective-permute-start.2 = (f32[4,256,128]{2,1,0:T(8,128)S(1)}, f32[4,256,128]{2,1,0:T(8,128)S(1)}, u32[]{:S(2)}, u32[]{:S(2)}) collective-permute-start(f32[4,256,128]{2,1,0:T(8,128)S(1)} %get-tuple-element.42.bot_ref), channel_id=1, source_target_pairs={{0,16},{16,32},{32,48},{48,64},{64,80},{80,96},{96,112},{112,128},... | collective-permute-start | bytes 1572872 | tf_op jit(solution)/shard_map/ppermute | solution.py:290
  22.7 28.3 %collective-permute-start.5 = (f32[4,256,128]{2,1,0:T(8,128)S(1)}, f32[4,256,128]{2,1,0:T(8,128)S(1)}, u32[]{:S(2)}, u32[]{:S(2)}) collective-permute-start(f32[4,256,128]{2,1,0:T(8,128)S(1)} %get-tuple-element.44.order_ref.top_ref), channel_id=1, source_target_pairs={{16,0},{32,16},{48,32},{64,48},{80,64},{96,80},{112,96},{128,112},... | collective-permute-start | bytes 1572872 | tf_op jit(solution)/shard_map/ppermute | solution.py:290
  26.5 24.5 %collective-permute-start.4 = (f32[4,256,128]{2,1,0:T(8,128)S(1)}, f32[4,256,128]{2,1,0:T(8,128)S(1)}, u32[]{:S(2)}, u32[]{:S(2)}) collective-permute-start(f32[4,256,128]{2,1,0:T(8,128)S(1)} %get-tuple-element.48.bot_ref), channel_id=1, source_target_pairs={{0,16},{16,32},{32,48},{48,64},{64,80},{80,96},{96,112},{112,128},... | collective-permute-start | bytes 1572872 | tf_op jit(solution)/shard_map/ppermute | solution.py:290
  31.7 46.1 %collective-permute-start.8 = (f32[4,256,128]{2,1,0:T(8,128)S(1)}, f32[4,256,128]{2,1,0:T(8,128)S(1)}, u32[]{:S(2)}, u32[]{:S(2)}) collective-permute-start(f32[4,256,128]{2,1,0:T(8,128)S(1)} %get-tuple-element.45.order_ref.top_ref), channel_id=1, source_target_pairs={{16,0},{32,16},{48,32},{64,48},{80,64},{96,80},{112,96},{128,112},... | collective-permute-start | bytes 1572872 | tf_op jit(solution)/shard_map/ppermute | solution.py:290
  35.6 42.3 %collective-permute-start.7 = (f32[4,256,128]{2,1,0:T(8,128)S(1)}, f32[4,256,128]{2,1,0:T(8,128)S(1)}, u32[]{:S(2)}, u32[]{:S(2)}) collective-permute-start(f32[4,256,128]{2,1,0:T(8,128)S(1)} %get-tuple-element.52.bot_ref), channel_id=1, source_target_pairs={{0,16},{16,32},{32,48},{48,64},{64,80},{80,96},{96,112},{112,128},... | collective-permute-start | bytes 1572872 | tf_op jit(solution)/shard_map/ppermute | solution.py:290
  52.9 39.9 %collective-permute-start.6 = (f32[4,32,8,128]{3,2,1,0:T(8,128)S(1)}, f32[4,32,8,128]{3,2,1,0:T(8,128)S(1)}, u32[]{:S(2)}, u32[]{:S(2)}) collective-permute-start(f32[4,32,8,128]{3,2,1,0:T(8,128)S(1)} %get-tuple-element.51), channel_id=1, source_target_pairs={{0,1},{1,0},{2,3},{3,2},{4,5},{5,4},{6,7},{7,6},{8,9},{9,8},{10,11... | collective-permute-start | bytes 1572872 | tf_op jit(solution)/shard_map/ppermute | solution.py:341
  71.8 35.2 %collective-permute-start.17 = (f32[4,256,128]{2,1,0:T(8,128)S(1)}, f32[4,256,128]{2,1,0:T(8,128)S(1)}, u32[]{:S(2)}, u32[]{:S(2)}) collective-permute-start(f32[4,256,128]{2,1,0:T(8,128)S(1)} %get-tuple-element.46.refs_0_.top_ref), channel_id=1, source_target_pairs={{16,0},{32,16},{48,32},{64,48},{80,64},{96,80},{112,96},{128,112},... | collective-permute-start | bytes 1572872 | tf_op jit(solution)/shard_map/ppermute | solution.py:290
  73.7 33.3 %collective-permute-start.16 = (f32[4,256,128]{2,1,0:T(8,128)S(1)}, f32[4,256,128]{2,1,0:T(8,128)S(1)}, u32[]{:S(2)}, u32[]{:S(2)}) collective-permute-start(f32[4,256,128]{2,1,0:T(8,128)S(1)} %get-tuple-element.63.bot_ref), channel_id=1, source_target_pairs={{0,16},{16,32},{32,48},{48,64},{64,80},{80,96},{96,112},{112,128},... | collective-permute-start | bytes 1572872 | tf_op jit(solution)/shard_map/ppermute | solution.py:290
  79.7 11.5 %collective-permute-start.10 = (f32[4,6,8,128]{3,2,1,0:T(8,128)S(1)}, f32[4,6,8,128]{3,2,1,0:T(8,128)S(1)}, u32[]{:S(2)}, u32[]{:S(2)}) collective-permute-start(f32[4,6,8,128]{3,2,1,0:T(8,128)S(1)} %get-tuple-element.56), channel_id=1, source_target_pairs={{0,1},{1,0},{2,3},{3,2},{4,5},{5,4},{6,7},{7,6},{8,9},{9,8},{10,11... | collective-permute-start | bytes 294920 | tf_op jit(solution)/shard_map/ppermute | solution.py:341
  90.2 1.3 collective-permute-start.11
  91.2 1.3 collective-permute-start.12
  91.5 1.3 collective-permute-start.9
  93.0 17.6 %collective-permute-start.13 = (f32[56,8,128]{2,1,0:T(8,128)S(1)}, f32[56,8,128]{2,1,0:T(8,128)S(1)}, u32[]{:S(2)}, u32[]{:S(2)}) collective-permute-start(f32[56,8,128]{2,1,0:T(8,128)S(1)} %get-tuple-element.60), channel_id=1, source_target_pairs={{0,4},{4,8},{8,12},{12,0},{1,5},{5,9},{9,13},{13,1},{2,6},{6,10},{... | collective-permute-start | bytes 688136 | tf_op jit(solution)/shard_map/ppermute | solution.py:358
  102.7 13.9 %collective-permute-start.14 = (f32[56,8,128]{2,1,0:T(8,128)S(1)}, f32[56,8,128]{2,1,0:T(8,128)S(1)}, u32[]{:S(2)}, u32[]{:S(2)}) collective-permute-start(f32[56,8,128]{2,1,0:T(8,128)S(1)} %get-tuple-element.61), channel_id=1, source_target_pairs={{0,8},{4,12},{8,0},{12,4},{1,9},{5,13},{9,1},{13,5},{2,10},{6,14},... | collective-permute-start | bytes 688136 | tf_op jit(solution)/shard_map/ppermute | solution.py:358
  105.9 10.7 %collective-permute-start.15 = (f32[56,8,128]{2,1,0:T(8,128)S(1)}, f32[56,8,128]{2,1,0:T(8,128)S(1)}, u32[]{:S(2)}, u32[]{:S(2)}) collective-permute-start(f32[56,8,128]{2,1,0:T(8,128)S(1)} %get-tuple-element.62), channel_id=1, source_target_pairs={{0,12},{4,0},{8,4},{12,8},{1,13},{5,1},{9,5},{13,9},{2,14},{6,2},{... | collective-permute-start | bytes 688136 | tf_op jit(solution)/shard_map/ppermute | solution.py:358
  118.0 3.0 %collective-permute-start.18 = (f32[4,75,8,128]{3,2,1,0:T(8,128)S(1)}, f32[4,75,8,128]{3,2,1,0:T(8,128)S(1)}, u32[]{:S(2)}, u32[]{:S(2)}) collective-permute-start(f32[4,75,8,128]{3,2,1,0:T(8,128)S(1)} %get-tuple-element.74), channel_id=1, source_target_pairs={{0,1},{1,0},{2,3},{3,2},{4,5},{5,4},{6,7},{7,6},{8,9},{9,8},{10,11... | collective-permute-start | bytes 3686408 | tf_op jit(solution)/shard_map/ppermute | solution.py:341

commit v3 on v2

--- a/solution.py
+++ b/solution.py
@@ -38,10 +38,11 @@
         for r in range(8):
             row = x_ref[g, pl.ds(r, 64, stride=8), :]
             slot = g * 32 + r * 4
-            here = (lane >= slot) & (lane < slot + 4)
-            left = jnp.where(here, pltpu.roll(row, slot, 1) if slot else row, left)
-            right = jnp.where(here, pltpu.roll(row, (slot + 4) % 128, 1), right)
-    left_ref[...] = left
+            after = (slot + 4) % 128
+            turned = pltpu.roll(row, after, 1) if after else row
+            right = jnp.where((lane >= slot) & (lane < slot + 4), turned, right)
+            left = jnp.where((lane >= after) & (lane < after + 4), turned, left)
+    left_ref[...] = pltpu.roll(left, 124, 1)
     right_ref[...] = right
 
 

time: 180 us -> 179 us (level)
  no operation moved by 1% of the time
where the time goes in v3:
time: 179 us
  starting transfers between devices  74.6 us (42%)
  blocking collectives  56.2 us (31%)
  Pallas kernels  26.6 us (15%)
  waiting for transfers between devices  20 us (11%)
    ppermute x10, starting transfers between devices, swap(): return (lax.ppermute(ahead, axes, up), lax.ppermute(back, axes, down))  30.4 us
    ppermute x6, starting transfers between devices, multiply(): lax.ppermute(piece, 'c', [(0, 1), (1, 0)])  30.2 us
    all_to_all x1, blocking collectives, local(): parts = [turns[0]] + moved + [lax.all_to_all(last, 'y', 0, 0, tiled=True)]  24.1 us
    all_to_all x1, blocking collectives, local(): part = lax.all_to_all(part, 'x', 0, 0, tiled=True)  18.6 us
    ppermute x3, starting transfers between devices, local(): lax.ppermute(turns[k], 'y', [(i, (i + k) % 4) for i in range(4)])  14.1 us
    all_to_all x1, blocking collectives, local(): part = lax.all_to_all(part, ('zl', 'zh'), 0, 0, tiled=True)  13.6 us
    pallas_call x4, Pallas kernels, smooth_rows(): pl.pallas_call(functools.partial(row_pass, start, count), grid=(1,), in_s...  12.6 us
    ppermute x3, waiting for transfers between devices, local(): lax.ppermute(turns[k], 'y', [(i, (i + k) % 4) for i in range(4)])  8.39 us
  transfers between devices with their start and end apart: 19, of which 8 were waited for; matrix products, arithmetic and copies ran while one was open for 0% of the time, Pallas kernels for 9%

profile of v3, /device:TPU:32, one launch (start us, length us, event | category | flops | bytes accessed | tf_op | source)
XLA Modules:
  0.0 178.6 jit_solution(15656380140681071465)
XLA Ops:
  0.0 4.6 %shard_map.17 = (f32[256,128]{1,0:T(8,128)}, f32[256,128]{1,0:T(8,128)}) custom-call(f32[4,2048,128]{2,1,0:T(8,128)} %bitcast.6), custom_call_target="tpu_custom_call" | custom-call | tf_op jit(solution)/shard_map/pallas_call | solution.py:293
  4.6 1.3 collective-permute-start.1
  5.9 3.0 %collective-permute-start = (f32[256,128]{1,0:T(8,128)}, f32[256,128]{1,0:T(8,128)S(1)}, u32[]{:S(2)}, u32[]{:S(2)}) collective-permute-start(f32[256,128]{1,0:T(8,128)} %get-tuple-element.40), channel_id=1, source_target_pairs={{0,1},{1,2},{2,3},{3,4},{4,5},{5,6},{6,7},{7,8},{8,9},{9,10},{10,1... | collective-permute-start | bytes 393224 | tf_op jit(solution)/shard_map/ppermute | solution.py:291
  8.9 0.9 copy-done
  9.9 0.2 collective-permute-done.left_ref
  10.1 3.1 %shard_map.19 = (f32[4,256,128]{2,1,0:T(8,128)S(1)}, f32[4,256,128]{2,1,0:T(8,128)S(1)}) custom-call(f32[8,1024,128]{2,1,0:T(8,128)} %bitcast.7, f32[256,128]{1,0:T(8,128)S(1)} %collective-permute-done.left_ref, f32[256,128]{1,0:T(8,128)S(1)} %collective-permute-done.1.right_ref, f32[8,256,128]{2,1,0:T(8,128)S(1)} %shard_map.18.w_ref, f32[256,128]{1,0:T(8,128)S(1)} %copy-done), custom_call_target="tpu_custom_call" | custom-call | tf_op jit(solution)/shard_map/pallas_call | solution.py:311
  13.2 3.8 %collective-permute-start.3 = (f32[4,256,128]{2,1,0:T(8,128)S(1)}, f32[4,256,128]{2,1,0:T(8,128)S(1)}, u32[]{:S(2)}, u32[]{:S(2)}) collective-permute-start(f32[4,256,128]{2,1,0:T(8,128)S(1)} %get-tuple-element.43.order_ref.top_ref), channel_id=1, source_target_pairs={{16,0},{32,16},{48,32},{64,48},{80,64},{96,80},{112,96},{128,112},... | collective-permute-start | bytes 1572872 | tf_op jit(solution)/shard_map/ppermute | solution.py:291
  17.0 2.1 %collective-permute-start.2 = (f32[4,256,128]{2,1,0:T(8,128)S(1)}, f32[4,256,128]{2,1,0:T(8,128)S(1)}, u32[]{:S(2)}, u32[]{:S(2)}) collective-permute-start(f32[4,256,128]{2,1,0:T(8,128)S(1)} %get-tuple-element.42.bot_ref), channel_id=1, source_target_pairs={{0,16},{16,32},{32,48},{48,64},{64,80},{80,96},{96,112},{112,128},... | collective-permute-start | bytes 1572872 | tf_op jit(solution)/shard_map/ppermute | solution.py:291
  19.1 3.1 %shard_map.20 = (f32[4,256,128]{2,1,0:T(8,128)S(1)}, f32[4,256,128]{2,1,0:T(8,128)S(1)}) custom-call(f32[8,1024,128]{2,1,0:T(8,128)} %bitcast.8, f32[256,128]{1,0:T(8,128)S(1)} %collective-permute-done.left_ref, f32[256,128]{1,0:T(8,128)S(1)} %collective-permute-done.1.right_ref, f32[8,256,128]{2,1,0:T(8,128)S(1)} %shard_map.18.w_ref, ...), custom_call_target="tpu_custom_call" | custom-call | tf_op jit(solution)/shard_map/pallas_call | solution.py:311
  22.2 3.8 %collective-permute-start.5 = (f32[4,256,128]{2,1,0:T(8,128)S(1)}, f32[4,256,128]{2,1,0:T(8,128)S(1)}, u32[]{:S(2)}, u32[]{:S(2)}) collective-permute-start(f32[4,256,128]{2,1,0:T(8,128)S(1)} %get-tuple-element.44.order_ref.top_ref), channel_id=1, source_target_pairs={{16,0},{32,16},{48,32},{64,48},{80,64},{96,80},{112,96},{128,112},... | collective-permute-start | bytes 1572872 | tf_op jit(solution)/shard_map/ppermute | solution.py:291
  26.0 2.1 %collective-permute-start.4 = (f32[4,256,128]{2,1,0:T(8,128)S(1)}, f32[4,256,128]{2,1,0:T(8,128)S(1)}, u32[]{:S(2)}, u32[]{:S(2)}) collective-permute-start(f32[4,256,128]{2,1,0:T(8,128)S(1)} %get-tuple-element.48.bot_ref), channel_id=1, source_target_pairs={{0,16},{16,32},{32,48},{48,64},{64,80},{80,96},{96,112},{112,128},... | collective-permute-start | bytes 1572872 | tf_op jit(solution)/shard_map/ppermute | solution.py:291
  28.1 3.2 %shard_map.21 = (f32[4,256,128]{2,1,0:T(8,128)S(1)}, f32[4,256,128]{2,1,0:T(8,128)S(1)}) custom-call(f32[8,1024,128]{2,1,0:T(8,128)} %bitcast.9, f32[256,128]{1,0:T(8,128)S(1)} %collective-permute-done.left_ref, f32[256,128]{1,0:T(8,128)S(1)} %collective-permute-done.1.right_ref, f32[8,256,128]{2,1,0:T(8,128)S(1)} %shard_map.18.w_ref, ...), custom_call_target="tpu_custom_call" | custom-call | tf_op jit(solution)/shard_map/pallas_call | solution.py:311
  31.3 3.8 %collective-permute-start.8 = (f32[4,256,128]{2,1,0:T(8,128)S(1)}, f32[4,256,128]{2,1,0:T(8,128)S(1)}, u32[]{:S(2)}, u32[]{:S(2)}) collective-permute-start(f32[4,256,128]{2,1,0:T(8,128)S(1)} %get-tuple-element.45.order_ref.top_ref), channel_id=1, source_target_pairs={{16,0},{32,16},{48,32},{64,48},{80,64},{96,80},{112,96},{128,112},... | collective-permute-start | bytes 1572872 | tf_op jit(solution)/shard_map/ppermute | solution.py:291
  35.1 4.5 %collective-permute-start.7 = (f32[4,256,128]{2,1,0:T(8,128)S(1)}, f32[4,256,128]{2,1,0:T(8,128)S(1)}, u32[]{:S(2)}, u32[]{:S(2)}) collective-permute-start(f32[4,256,128]{2,1,0:T(8,128)S(1)} %get-tuple-element.52.bot_ref), channel_id=1, source_target_pairs={{0,16},{16,32},{32,48},{48,64},{64,80},{80,96},{96,112},{112,128},... | collective-permute-start | bytes 1572872 | tf_op jit(solution)/shard_map/ppermute | solution.py:291
  39.6 3.2 %shard_map.22 = (f32[4,256,128]{2,1,0:T(8,128)S(1)}, f32[4,256,128]{2,1,0:T(8,128)S(1)}) custom-call(f32[8,1024,128]{2,1,0:T(8,128)} %bitcast.10, f32[256,128]{1,0:T(8,128)S(1)} %collective-permute-done.left_ref, f32[256,128]{1,0:T(8,128)S(1)} %collective-permute-done.1.right_ref, f32[8,256,128]{2,1,0:T(8,128)S(1)} %shard_map.18.w_ref, ...), custom_call_target="tpu_custom_call" | custom-call | tf_op jit(solution)/shard_map/pallas_call | solution.py:311
  42.8 1.2 shard_map.23
  44.0 6.5 %collective-permute-done.5.below_ref = f32[4,256,128]{2,1,0:T(8,128)S(1)} collective-permute-done((f32[4,256,128]{2,1,0:T(8,128)S(1)}, f32[4,256,128]{2,1,0:T(8,128)S(1)}, u32[]{:S(2)}, u32[]{:S(2)}) %collective-permute-start.5) | collective-permute-done | bytes 524320 | tf_op jit(solution)/shard_map/ppermute | solution.py:291
  50.5 1.2 shard_map.24
  51.7 0.8 shard_map.25
  52.4 18.9 %collective-permute-start.6 = (f32[4,32,8,128]{3,2,1,0:T(8,128)S(1)}, f32[4,32,8,128]{3,2,1,0:T(8,128)S(1)}, u32[]{:S(2)}, u32[]{:S(2)}) collective-permute-start(f32[4,32,8,128]{3,2,1,0:T(8,128)S(1)} %get-tuple-element.51), channel_id=1, source_target_pairs={{0,1},{1,0},{2,3},{3,2},{4,5},{5,4},{6,7},{7,6},{8,9},{9,8},{10,11... | collective-permute-start | bytes 1572872 | tf_op jit(solution)/shard_map/ppermute | solution.py:342
  71.3 1.9 %collective-permute-start.17 = (f32[4,256,128]{2,1,0:T(8,128)S(1)}, f32[4,256,128]{2,1,0:T(8,128)S(1)}, u32[]{:S(2)}, u32[]{:S(2)}) collective-permute-start(f32[4,256,128]{2,1,0:T(8,128)S(1)} %get-tuple-element.46.refs_0_.top_ref), channel_id=1, source_target_pairs={{16,0},{32,16},{48,32},{64,48},{80,64},{96,80},{112,96},{128,112},... | collective-permute-start | bytes 1572872 | tf_op jit(solution)/shard_map/ppermute | solution.py:291
  73.3 4.1 %collective-permute-start.16 = (f32[4,256,128]{2,1,0:T(8,128)S(1)}, f32[4,256,128]{2,1,0:T(8,128)S(1)}, u32[]{:S(2)}, u32[]{:S(2)}) collective-permute-start(f32[4,256,128]{2,1,0:T(8,128)S(1)} %get-tuple-element.63.bot_ref), channel_id=1, source_target_pairs={{0,16},{16,32},{32,48},{48,64},{64,80},{80,96},{96,112},{112,128},... | collective-permute-start | bytes 1572872 | tf_op jit(solution)/shard_map/ppermute | solution.py:291
  77.4 1.2 shard_map.26
  78.5 0.6 shard_map.27
  79.2 10.6 %collective-permute-start.10 = (f32[4,6,8,128]{3,2,1,0:T(8,128)S(1)}, f32[4,6,8,128]{3,2,1,0:T(8,128)S(1)}, u32[]{:S(2)}, u32[]{:S(2)}) collective-permute-start(f32[4,6,8,128]{3,2,1,0:T(8,128)S(1)} %get-tuple-element.56), channel_id=1, source_target_pairs={{0,1},{1,0},{2,3},{3,2},{4,5},{5,4},{6,7},{7,6},{8,9},{9,8},{10,11... | collective-permute-start | bytes 294920 | tf_op jit(solution)/shard_map/ppermute | solution.py:342
  89.7 0.1 collective-permute-start.11
  89.8 0.8 collective-permute-done.10.refs_1_
  90.7 0.4 collective-permute-start.12
  91.1 0.2 collective-permute-start.9
  91.2 0.8 collective-permute-done.12.refs_3_
  92.0 0.4 collective-permute-done.9.refs_0_
  92.4 0.1 shard_map.28
  92.5 9.7 %collective-permute-start.13 = (f32[56,8,128]{2,1,0:T(8,128)S(1)}, f32[56,8,128]{2,1,0:T(8,128)S(1)}, u32[]{:S(2)}, u32[]{:S(2)}) collective-permute-start(f32[56,8,128]{2,1,0:T(8,128)S(1)} %get-tuple-element.60), channel_id=1, source_target_pairs={{0,4},{4,8},{8,12},{12,0},{1,5},{5,9},{9,13},{13,1},{2,6},{6,10},{... | collective-permute-start | bytes 688136 | tf_op jit(solution)/shard_map/ppermute | solution.py:359
  102.2 3.2 %collective-permute-start.14 = (f32[56,8,128]{2,1,0:T(8,128)S(1)}, f32[56,8,128]{2,1,0:T(8,128)S(1)}, u32[]{:S(2)}, u32[]{:S(2)}) collective-permute-start(f32[56,8,128]{2,1,0:T(8,128)S(1)} %get-tuple-element.61), channel_id=1, source_target_pairs={{0,8},{4,12},{8,0},{12,4},{1,9},{5,13},{9,1},{13,5},{2,10},{6,14},... | collective-permute-start | bytes 688136 | tf_op jit(solution)/shard_map/ppermute | solution.py:359
  105.4 1.2 collective-permute-start.15
  106.5 1.2 shard_map.29
  107.7 2.3 %collective-permute-done.13.refs_6_.refs_1_ = f32[56,8,128]{2,1,0:T(8,128)S(1)} collective-permute-done((f32[56,8,128]{2,1,0:T(8,128)S(1)}, f32[56,8,128]{2,1,0:T(8,128)S(1)}, u32[]{:S(2)}, u32[]{:S(2)}) %collective-permute-start.13) | collective-permute-done | bytes 229408 | tf_op jit(solution)/shard_map/ppermute | solution.py:359
  110.0 6.1 %collective-permute-done.14.refs_7_.refs_2_ = f32[56,8,128]{2,1,0:T(8,128)S(1)} collective-permute-done((f32[56,8,128]{2,1,0:T(8,128)S(1)}, f32[56,8,128]{2,1,0:T(8,128)S(1)}, u32[]{:S(2)}, u32[]{:S(2)}) %collective-permute-start.14) | collective-permute-done | bytes 229408 | tf_op jit(solution)/shard_map/ppermute | solution.py:359
  116.1 1.4 shard_map.30
  117.6 0.1 collective-permute-start.18
  117.7 2.9 %collective-permute-done.18.refs_1_ = f32[4,75,8,128]{3,2,1,0:T(8,128)S(1)} collective-permute-done((f32[4,75,8,128]{3,2,1,0:T(8,128)S(1)}, f32[4,75,8,128]{3,2,1,0:T(8,128)S(1)}, u32[]{:S(2)}, u32[]{:S(2)}) %collective-permute-start.18) | collective-permute-done | bytes 1228832 | tf_op jit(solution)/shard_map/ppermute | solution.py:342
  120.6 0.2 shard_map.31
  120.7 24.1 %all_to_all.15.refs_4_ = f32[4,75,8,128]{3,2,1,0:T(8,128)S(1)} all-to-all(f32[4,75,8,128]{3,2,1,0:T(8,128)S(1)} %shard_map.31), channel_id=1, replica_groups=mesh['x'=4,'zl'=4,'y'=4,'zh'=2,'c'=2] {'y'}, dimensions={0} | all-to-all | bytes 2457600 | tf_op jit(solution)/shard_map/all_to_all | solution.py:371
  144.8 0.1 shard_map.32
  144.9 18.6 %all_to_all.16.part_ref = f32[4,41,8,128]{3,2,1,0:T(8,128)S(1)} all-to-all(f32[4,41,8,128]{3,2,1,0:T(8,128)S(1)} %shard_map.32), channel_id=1, replica_groups=mesh['x'=4,'zl'=4,'y'=4,'zh'=2,'c'=2] {'x'}, dimensions={0} | all-to-all | bytes 1343488 | tf_op jit(solution)/shard_map/all_to_all | solution.py:380
  163.5 0.5 shard_map.33
  164.0 13.6 %all_to_all.17.part_ref = f32[8,6,8,128]{3,2,1,0:T(8,128)S(1)} all-to-all(f32[8,6,8,128]{3,2,1,0:T(8,128)S(1)} %shard_map.33), channel_id=1, replica_groups=mesh['x'=4,'zl'=4,'y'=4,'zh'=2,'c'=2] {'zl','zh'}, dimensions={0} | all-to-all | bytes 393216 | tf_op jit(solution)/shard_map/all_to_all | solution.py:389
  177.6 1.0 shard_map.34
  (14 shorter events, 0.1 us)
Async XLA Ops:
  4.6 5.3 %collective-permute-start.1 = (f32[256,128]{1,0:T(8,128)}, f32[256,128]{1,0:T(8,128)S(1)}, u32[]{:S(2)}, u32[]{:S(2)}) collective-permute-start(f32[256,128]{1,0:T(8,128)} %get-tuple-element.41.order_ref), channel_id=1, source_target_pairs={{1,0},{2,1},{3,2},{4,3},{5,4},{6,5},{7,6},{8,7},{9,8},{10,9},{11,1... | collective-permute-start | bytes 393224 | tf_op jit(solution)/shard_map/ppermute | solution.py:291
  5.9 4.2 %collective-permute-start = (f32[256,128]{1,0:T(8,128)}, f32[256,128]{1,0:T(8,128)S(1)}, u32[]{:S(2)}, u32[]{:S(2)}) collective-permute-start(f32[256,128]{1,0:T(8,128)} %get-tuple-element.40), channel_id=1, source_target_pairs={{0,1},{1,2},{2,3},{3,4},{4,5},{5,6},{6,7},{7,8},{8,9},{9,10},{10,1... | collective-permute-start | bytes 393224 | tf_op jit(solution)/shard_map/ppermute | solution.py:291
  8.9 0.9 copy-start
  13.2 21.9 %collective-permute-start.3 = (f32[4,256,128]{2,1,0:T(8,128)S(1)}, f32[4,256,128]{2,1,0:T(8,128)S(1)}, u32[]{:S(2)}, u32[]{:S(2)}) collective-permute-start(f32[4,256,128]{2,1,0:T(8,128)S(1)} %get-tuple-element.43.order_ref.top_ref), channel_id=1, source_target_pairs={{16,0},{32,16},{48,32},{64,48},{80,64},{96,80},{112,96},{128,112},... | collective-permute-start | bytes 1572872 | tf_op jit(solution)/shard_map/ppermute | solution.py:291
  17.0 25.8 %collective-permute-start.2 = (f32[4,256,128]{2,1,0:T(8,128)S(1)}, f32[4,256,128]{2,1,0:T(8,128)S(1)}, u32[]{:S(2)}, u32[]{:S(2)}) collective-permute-start(f32[4,256,128]{2,1,0:T(8,128)S(1)} %get-tuple-element.42.bot_ref), channel_id=1, source_target_pairs={{0,16},{16,32},{32,48},{48,64},{64,80},{80,96},{96,112},{112,128},... | collective-permute-start | bytes 1572872 | tf_op jit(solution)/shard_map/ppermute | solution.py:291
  22.2 28.3 %collective-permute-start.5 = (f32[4,256,128]{2,1,0:T(8,128)S(1)}, f32[4,256,128]{2,1,0:T(8,128)S(1)}, u32[]{:S(2)}, u32[]{:S(2)}) collective-permute-start(f32[4,256,128]{2,1,0:T(8,128)S(1)} %get-tuple-element.44.order_ref.top_ref), channel_id=1, source_target_pairs={{16,0},{32,16},{48,32},{64,48},{80,64},{96,80},{112,96},{128,112},... | collective-permute-start | bytes 1572872 | tf_op jit(solution)/shard_map/ppermute | solution.py:291
  26.0 24.5 %collective-permute-start.4 = (f32[4,256,128]{2,1,0:T(8,128)S(1)}, f32[4,256,128]{2,1,0:T(8,128)S(1)}, u32[]{:S(2)}, u32[]{:S(2)}) collective-permute-start(f32[4,256,128]{2,1,0:T(8,128)S(1)} %get-tuple-element.48.bot_ref), channel_id=1, source_target_pairs={{0,16},{16,32},{32,48},{48,64},{64,80},{80,96},{96,112},{112,128},... | collective-permute-start | bytes 1572872 | tf_op jit(solution)/shard_map/ppermute | solution.py:291
  31.3 46.1 %collective-permute-start.8 = (f32[4,256,128]{2,1,0:T(8,128)S(1)}, f32[4,256,128]{2,1,0:T(8,128)S(1)}, u32[]{:S(2)}, u32[]{:S(2)}) collective-permute-start(f32[4,256,128]{2,1,0:T(8,128)S(1)} %get-tuple-element.45.order_ref.top_ref), channel_id=1, source_target_pairs={{16,0},{32,16},{48,32},{64,48},{80,64},{96,80},{112,96},{128,112},... | collective-permute-start | bytes 1572872 | tf_op jit(solution)/shard_map/ppermute | solution.py:291
  35.1 42.3 %collective-permute-start.7 = (f32[4,256,128]{2,1,0:T(8,128)S(1)}, f32[4,256,128]{2,1,0:T(8,128)S(1)}, u32[]{:S(2)}, u32[]{:S(2)}) collective-permute-start(f32[4,256,128]{2,1,0:T(8,128)S(1)} %get-tuple-element.52.bot_ref), channel_id=1, source_target_pairs={{0,16},{16,32},{32,48},{48,64},{64,80},{80,96},{96,112},{112,128},... | collective-permute-start | bytes 1572872 | tf_op jit(solution)/shard_map/ppermute | solution.py:291
  52.4 39.9 %collective-permute-start.6 = (f32[4,32,8,128]{3,2,1,0:T(8,128)S(1)}, f32[4,32,8,128]{3,2,1,0:T(8,128)S(1)}, u32[]{:S(2)}, u32[]{:S(2)}) collective-permute-start(f32[4,32,8,128]{3,2,1,0:T(8,128)S(1)} %get-tuple-element.51), channel_id=1, source_target_pairs={{0,1},{1,0},{2,3},{3,2},{4,5},{5,4},{6,7},{7,6},{8,9},{9,8},{10,11... | collective-permute-start | bytes 1572872 | tf_op jit(solution)/shard_map/ppermute | solution.py:342
  71.3 35.2 %collective-permute-start.17 = (f32[4,256,128]{2,1,0:T(8,128)S(1)}, f32[4,256,128]{2,1,0:T(8,128)S(1)}, u32[]{:S(2)}, u32[]{:S(2)}) collective-permute-start(f32[4,256,128]{2,1,0:T(8,128)S(1)} %get-tuple-element.46.refs_0_.top_ref), channel_id=1, source_target_pairs={{16,0},{32,16},{48,32},{64,48},{80,64},{96,80},{112,96},{128,112},... | collective-permute-start | bytes 1572872 | tf_op jit(solution)/shard_map/ppermute | solution.py:291
  73.3 33.3 %collective-permute-start.16 = (f32[4,256,128]{2,1,0:T(8,128)S(1)}, f32[4,256,128]{2,1,0:T(8,128)S(1)}, u32[]{:S(2)}, u32[]{:S(2)}) collective-permute-start(f32[4,256,128]{2,1,0:T(8,128)S(1)} %get-tuple-element.63.bot_ref), channel_id=1, source_target_pairs={{0,16},{16,32},{32,48},{48,64},{64,80},{80,96},{96,112},{112,128},... | collective-permute-start | bytes 1572872 | tf_op jit(solution)/shard_map/ppermute | solution.py:291
  79.2 11.5 %collective-permute-start.10 = (f32[4,6,8,128]{3,2,1,0:T(8,128)S(1)}, f32[4,6,8,128]{3,2,1,0:T(8,128)S(1)}, u32[]{:S(2)}, u32[]{:S(2)}) collective-permute-start(f32[4,6,8,128]{3,2,1,0:T(8,128)S(1)} %get-tuple-element.56), channel_id=1, source_target_pairs={{0,1},{1,0},{2,3},{3,2},{4,5},{5,4},{6,7},{7,6},{8,9},{9,8},{10,11... | collective-permute-start | bytes 294920 | tf_op jit(solution)/shard_map/ppermute | solution.py:342
  89.7 1.3 collective-permute-start.11
  90.7 1.3 collective-permute-start.12
  91.1 1.3 collective-permute-start.9
  92.5 17.5 %collective-permute-start.13 = (f32[56,8,128]{2,1,0:T(8,128)S(1)}, f32[56,8,128]{2,1,0:T(8,128)S(1)}, u32[]{:S(2)}, u32[]{:S(2)}) collective-permute-start(f32[56,8,128]{2,1,0:T(8,128)S(1)} %get-tuple-element.60), channel_id=1, source_target_pairs={{0,4},{4,8},{8,12},{12,0},{1,5},{5,9},{9,13},{13,1},{2,6},{6,10},{... | collective-permute-start | bytes 688136 | tf_op jit(solution)/shard_map/ppermute | solution.py:359
  102.2 13.9 %collective-permute-start.14 = (f32[56,8,128]{2,1,0:T(8,128)S(1)}, f32[56,8,128]{2,1,0:T(8,128)S(1)}, u32[]{:S(2)}, u32[]{:S(2)}) collective-permute-start(f32[56,8,128]{2,1,0:T(8,128)S(1)} %get-tuple-element.61), channel_id=1, source_target_pairs={{0,8},{4,12},{8,0},{12,4},{1,9},{5,13},{9,1},{13,5},{2,10},{6,14},... | collective-permute-start | bytes 688136 | tf_op jit(solution)/shard_map/ppermute | solution.py:359
  105.4 10.7 %collective-permute-start.15 = (f32[56,8,128]{2,1,0:T(8,128)S(1)}, f32[56,8,128]{2,1,0:T(8,128)S(1)}, u32[]{:S(2)}, u32[]{:S(2)}) collective-permute-start(f32[56,8,128]{2,1,0:T(8,128)S(1)} %get-tuple-element.62), channel_id=1, source_target_pairs={{0,12},{4,0},{8,4},{12,8},{1,13},{5,1},{9,5},{13,9},{2,14},{6,2},{... | collective-permute-start | bytes 688136 | tf_op jit(solution)/shard_map/ppermute | solution.py:359
  117.6 3.0 %collective-permute-start.18 = (f32[4,75,8,128]{3,2,1,0:T(8,128)S(1)}, f32[4,75,8,128]{3,2,1,0:T(8,128)S(1)}, u32[]{:S(2)}, u32[]{:S(2)}) collective-permute-start(f32[4,75,8,128]{3,2,1,0:T(8,128)S(1)} %get-tuple-element.74), channel_id=1, source_target_pairs={{0,1},{1,0},{2,3},{3,2},{4,5},{5,4},{6,7},{7,6},{8,9},{9,8},{10,11... | collective-permute-start | bytes 3686408 | tf_op jit(solution)/shard_map/ppermute | solution.py:342

commit v4 on v3

--- a/solution.py
+++ b/solution.py
@@ -76,17 +76,14 @@
 
 
 def row_pass(start, count, x_ref, left_ref, right_ref, w_ref, order_ref, top_ref, bot_ref):
-    for part in range(count):
-        at = slice(part * 128, (part + 1) * 128)
-        group, half = divmod(start + part, 2)
-        edge = slice(half * 128, half * 128 + 128)
-        halo = halo_lanes(group, left_ref[edge], right_ref[edge])
-        for r in range(8):
-            smooth = smooth_row(x_ref[part, pl.ds(r, 128, stride=8), :], halo, w_ref[r])
-            if r < 4:
-                top_ref[r, at] = smooth
-            else:
-                bot_ref[r - 4, at] = smooth
+    halo = halo_lanes(start // 2, left_ref[...], right_ref[...])
+    for r in range(8):
+        row = jnp.concatenate([x_ref[part, pl.ds(r, 128, stride=8), :] for part in range(count)], axis=0)
+        smooth = smooth_row(row, halo, w_ref[r])
+        if r < 4:
+            top_ref[r] = smooth
+        else:
+            bot_ref[r - 4] = smooth
 
 
 def to_lanes(squares, level):

time: 179 us -> 179 us (level)
  no operation moved by 1% of the time
where the time goes in v4:
time: 179 us
  starting transfers between devices  74.6 us (42%)
  blocking collectives  56.3 us (31%)
  Pallas kernels  26.3 us (15%)
  waiting for transfers between devices  20.2 us (11%)
    ppermute x6, starting transfers between devices, multiply(): lax.ppermute(piece, 'c', [(0, 1), (1, 0)])  30.7 us
    ppermute x10, starting transfers between devices, swap(): return (lax.ppermute(ahead, axes, up), lax.ppermute(back, axes, down))  30.2 us
    all_to_all x1, blocking collectives, local(): parts = [turns[0]] + moved + [lax.all_to_all(last, 'y', 0, 0, tiled=True)]  24.2 us
    all_to_all x1, blocking collectives, local(): part = lax.all_to_all(part, 'x', 0, 0, tiled=True)  18.5 us
    ppermute x3, starting transfers between devices, local(): lax.ppermute(turns[k], 'y', [(i, (i + k) % 4) for i in range(4)])  13.7 us
    all_to_all x1, blocking collectives, local(): part = lax.all_to_all(part, ('zl', 'zh'), 0, 0, tiled=True)  13.6 us
    pallas_call x4, Pallas kernels, smooth_rows(): pl.pallas_call(functools.partial(row_pass, start, count), grid=(1,), in_s...  12.3 us
    ppermute x3, waiting for transfers between devices, local(): lax.ppermute(turns[k], 'y', [(i, (i + k) % 4) for i in range(4)])  8.28 us
  transfers between devices with their start and end apart: 19, of which 8 were waited for; matrix products, arithmetic and copies ran while one was open for 0% of the time, Pallas kernels for 9%

profile of v4, /device:TPU:32, one launch (start us, length us, event | category | flops | bytes accessed | tf_op | source)
XLA Modules:
  0.0 178.5 jit_solution(9984987081793788495)
XLA Ops:
  0.0 4.6 %shard_map.17 = (f32[256,128]{1,0:T(8,128)}, f32[256,128]{1,0:T(8,128)}) custom-call(f32[4,2048,128]{2,1,0:T(8,128)} %bitcast.6), custom_call_target="tpu_custom_call" | custom-call | tf_op jit(solution)/shard_map/pallas_call | solution.py:290
  4.6 1.3 collective-permute-start.1
  5.9 3.0 %collective-permute-start = (f32[256,128]{1,0:T(8,128)}, f32[256,128]{1,0:T(8,128)S(1)}, u32[]{:S(2)}, u32[]{:S(2)}) collective-permute-start(f32[256,128]{1,0:T(8,128)} %get-tuple-element.40), channel_id=1, source_target_pairs={{0,1},{1,2},{2,3},{3,4},{4,5},{5,6},{6,7},{7,8},{8,9},{9,10},{10,1... | collective-permute-start | bytes 393224 | tf_op jit(solution)/shard_map/ppermute | solution.py:288
  8.9 0.9 copy-done
  9.9 0.2 collective-permute-done.left_ref
  10.1 3.1 %shard_map.19 = (f32[4,256,128]{2,1,0:T(8,128)S(1)}, f32[4,256,128]{2,1,0:T(8,128)S(1)}) custom-call(f32[8,1024,128]{2,1,0:T(8,128)} %bitcast.7, f32[256,128]{1,0:T(8,128)S(1)} %collective-permute-done.left_ref, f32[256,128]{1,0:T(8,128)S(1)} %collective-permute-done.1.right_ref, f32[8,256,128]{2,1,0:T(8,128)S(1)} %shard_map.18.w_ref, f32[256,128]{1,0:T(8,128)S(1)} %copy-done), custom_call_target="tpu_custom_call" | custom-call | tf_op jit(solution)/shard_map/pallas_call | solution.py:308
  13.1 3.8 %collective-permute-start.3 = (f32[4,256,128]{2,1,0:T(8,128)S(1)}, f32[4,256,128]{2,1,0:T(8,128)S(1)}, u32[]{:S(2)}, u32[]{:S(2)}) collective-permute-start(f32[4,256,128]{2,1,0:T(8,128)S(1)} %get-tuple-element.43.order_ref.top_ref), channel_id=1, source_target_pairs={{16,0},{32,16},{48,32},{64,48},{80,64},{96,80},{112,96},{128,112},... | collective-permute-start | bytes 1572872 | tf_op jit(solution)/shard_map/ppermute | solution.py:288
  16.9 2.1 %collective-permute-start.2 = (f32[4,256,128]{2,1,0:T(8,128)S(1)}, f32[4,256,128]{2,1,0:T(8,128)S(1)}, u32[]{:S(2)}, u32[]{:S(2)}) collective-permute-start(f32[4,256,128]{2,1,0:T(8,128)S(1)} %get-tuple-element.42.bot_ref), channel_id=1, source_target_pairs={{0,16},{16,32},{32,48},{48,64},{64,80},{80,96},{96,112},{112,128},... | collective-permute-start | bytes 1572872 | tf_op jit(solution)/shard_map/ppermute | solution.py:288
  19.0 3.1 %shard_map.20 = (f32[4,256,128]{2,1,0:T(8,128)S(1)}, f32[4,256,128]{2,1,0:T(8,128)S(1)}) custom-call(f32[8,1024,128]{2,1,0:T(8,128)} %bitcast.8, f32[256,128]{1,0:T(8,128)S(1)} %collective-permute-done.left_ref, f32[256,128]{1,0:T(8,128)S(1)} %collective-permute-done.1.right_ref, f32[8,256,128]{2,1,0:T(8,128)S(1)} %shard_map.18.w_ref, ...), custom_call_target="tpu_custom_call" | custom-call | tf_op jit(solution)/shard_map/pallas_call | solution.py:308
  22.1 3.8 %collective-permute-start.5 = (f32[4,256,128]{2,1,0:T(8,128)S(1)}, f32[4,256,128]{2,1,0:T(8,128)S(1)}, u32[]{:S(2)}, u32[]{:S(2)}) collective-permute-start(f32[4,256,128]{2,1,0:T(8,128)S(1)} %get-tuple-element.44.order_ref.top_ref), channel_id=1, source_target_pairs={{16,0},{32,16},{48,32},{64,48},{80,64},{96,80},{112,96},{128,112},... | collective-permute-start | bytes 1572872 | tf_op jit(solution)/shard_map/ppermute | solution.py:288
  25.9 2.1 %collective-permute-start.4 = (f32[4,256,128]{2,1,0:T(8,128)S(1)}, f32[4,256,128]{2,1,0:T(8,128)S(1)}, u32[]{:S(2)}, u32[]{:S(2)}) collective-permute-start(f32[4,256,128]{2,1,0:T(8,128)S(1)} %get-tuple-element.48.bot_ref), channel_id=1, source_target_pairs={{0,16},{16,32},{32,48},{48,64},{64,80},{80,96},{96,112},{112,128},... | collective-permute-start | bytes 1572872 | tf_op jit(solution)/shard_map/ppermute | solution.py:288
  27.9 3.1 %shard_map.21 = (f32[4,256,128]{2,1,0:T(8,128)S(1)}, f32[4,256,128]{2,1,0:T(8,128)S(1)}) custom-call(f32[8,1024,128]{2,1,0:T(8,128)} %bitcast.9, f32[256,128]{1,0:T(8,128)S(1)} %collective-permute-done.left_ref, f32[256,128]{1,0:T(8,128)S(1)} %collective-permute-done.1.right_ref, f32[8,256,128]{2,1,0:T(8,128)S(1)} %shard_map.18.w_ref, ...), custom_call_target="tpu_custom_call" | custom-call | tf_op jit(solution)/shard_map/pallas_call | solution.py:308
  31.0 3.8 %collective-permute-start.8 = (f32[4,256,128]{2,1,0:T(8,128)S(1)}, f32[4,256,128]{2,1,0:T(8,128)S(1)}, u32[]{:S(2)}, u32[]{:S(2)}) collective-permute-start(f32[4,256,128]{2,1,0:T(8,128)S(1)} %get-tuple-element.45.order_ref.top_ref), channel_id=1, source_target_pairs={{16,0},{32,16},{48,32},{64,48},{80,64},{96,80},{112,96},{128,112},... | collective-permute-start | bytes 1572872 | tf_op jit(solution)/shard_map/ppermute | solution.py:288
  34.8 4.5 %collective-permute-start.7 = (f32[4,256,128]{2,1,0:T(8,128)S(1)}, f32[4,256,128]{2,1,0:T(8,128)S(1)}, u32[]{:S(2)}, u32[]{:S(2)}) collective-permute-start(f32[4,256,128]{2,1,0:T(8,128)S(1)} %get-tuple-element.52.bot_ref), channel_id=1, source_target_pairs={{0,16},{16,32},{32,48},{48,64},{64,80},{80,96},{96,112},{112,128},... | collective-permute-start | bytes 1572872 | tf_op jit(solution)/shard_map/ppermute | solution.py:288
  39.4 3.1 %shard_map.22 = (f32[4,256,128]{2,1,0:T(8,128)S(1)}, f32[4,256,128]{2,1,0:T(8,128)S(1)}) custom-call(f32[8,1024,128]{2,1,0:T(8,128)} %bitcast.10, f32[256,128]{1,0:T(8,128)S(1)} %collective-permute-done.left_ref, f32[256,128]{1,0:T(8,128)S(1)} %collective-permute-done.1.right_ref, f32[8,256,128]{2,1,0:T(8,128)S(1)} %shard_map.18.w_ref, ...), custom_call_target="tpu_custom_call" | custom-call | tf_op jit(solution)/shard_map/pallas_call | solution.py:308
  42.5 1.2 shard_map.23
  43.6 7.1 %collective-permute-done.5.below_ref = f32[4,256,128]{2,1,0:T(8,128)S(1)} collective-permute-done((f32[4,256,128]{2,1,0:T(8,128)S(1)}, f32[4,256,128]{2,1,0:T(8,128)S(1)}, u32[]{:S(2)}, u32[]{:S(2)}) %collective-permute-start.5) | collective-permute-done | bytes 524320 | tf_op jit(solution)/shard_map/ppermute | solution.py:288
  50.8 1.2 shard_map.24
  51.9 0.8 shard_map.25
  52.7 18.6 %collective-permute-start.6 = (f32[4,32,8,128]{3,2,1,0:T(8,128)S(1)}, f32[4,32,8,128]{3,2,1,0:T(8,128)S(1)}, u32[]{:S(2)}, u32[]{:S(2)}) collective-permute-start(f32[4,32,8,128]{3,2,1,0:T(8,128)S(1)} %get-tuple-element.51), channel_id=1, source_target_pairs={{0,1},{1,0},{2,3},{3,2},{4,5},{5,4},{6,7},{7,6},{8,9},{9,8},{10,11... | collective-permute-start | bytes 1572872 | tf_op jit(solution)/shard_map/ppermute | solution.py:339
  71.2 1.9 %collective-permute-start.17 = (f32[4,256,128]{2,1,0:T(8,128)S(1)}, f32[4,256,128]{2,1,0:T(8,128)S(1)}, u32[]{:S(2)}, u32[]{:S(2)}) collective-permute-start(f32[4,256,128]{2,1,0:T(8,128)S(1)} %get-tuple-element.46.refs_0_.top_ref), channel_id=1, source_target_pairs={{16,0},{32,16},{48,32},{64,48},{80,64},{96,80},{112,96},{128,112},... | collective-permute-start | bytes 1572872 | tf_op jit(solution)/shard_map/ppermute | solution.py:288
  73.2 3.9 %collective-permute-start.16 = (f32[4,256,128]{2,1,0:T(8,128)S(1)}, f32[4,256,128]{2,1,0:T(8,128)S(1)}, u32[]{:S(2)}, u32[]{:S(2)}) collective-permute-start(f32[4,256,128]{2,1,0:T(8,128)S(1)} %get-tuple-element.63.bot_ref), channel_id=1, source_target_pairs={{0,16},{16,32},{32,48},{48,64},{64,80},{80,96},{96,112},{112,128},... | collective-permute-start | bytes 1572872 | tf_op jit(solution)/shard_map/ppermute | solution.py:288
  77.1 1.2 shard_map.26
  78.3 0.6 shard_map.27
  78.9 11.1 %collective-permute-start.10 = (f32[4,6,8,128]{3,2,1,0:T(8,128)S(1)}, f32[4,6,8,128]{3,2,1,0:T(8,128)S(1)}, u32[]{:S(2)}, u32[]{:S(2)}) collective-permute-start(f32[4,6,8,128]{3,2,1,0:T(8,128)S(1)} %get-tuple-element.56), channel_id=1, source_target_pairs={{0,1},{1,0},{2,3},{3,2},{4,5},{5,4},{6,7},{7,6},{8,9},{9,8},{10,11... | collective-permute-start | bytes 294920 | tf_op jit(solution)/shard_map/ppermute | solution.py:339
  90.0 0.3 collective-permute-start.11
  90.3 0.7 collective-permute-done.10.refs_1_
  91.0 0.4 collective-permute-start.12
  91.3 0.3 collective-permute-start.9
  91.6 0.7 collective-permute-done.12.refs_3_
  92.3 0.4 collective-permute-done.9.refs_0_
  92.6 0.1 shard_map.28
  92.7 9.4 %collective-permute-start.13 = (f32[56,8,128]{2,1,0:T(8,128)S(1)}, f32[56,8,128]{2,1,0:T(8,128)S(1)}, u32[]{:S(2)}, u32[]{:S(2)}) collective-permute-start(f32[56,8,128]{2,1,0:T(8,128)S(1)} %get-tuple-element.60), channel_id=1, source_target_pairs={{0,4},{4,8},{8,12},{12,0},{1,5},{5,9},{9,13},{13,1},{2,6},{6,10},{... | collective-permute-start | bytes 688136 | tf_op jit(solution)/shard_map/ppermute | solution.py:356
  102.1 3.2 %collective-permute-start.14 = (f32[56,8,128]{2,1,0:T(8,128)S(1)}, f32[56,8,128]{2,1,0:T(8,128)S(1)}, u32[]{:S(2)}, u32[]{:S(2)}) collective-permute-start(f32[56,8,128]{2,1,0:T(8,128)S(1)} %get-tuple-element.61), channel_id=1, source_target_pairs={{0,8},{4,12},{8,0},{12,4},{1,9},{5,13},{9,1},{13,5},{2,10},{6,14},... | collective-permute-start | bytes 688136 | tf_op jit(solution)/shard_map/ppermute | solution.py:356
  105.3 1.2 collective-permute-start.15
  106.5 1.2 shard_map.29
  107.7 2.2 %collective-permute-done.13.refs_6_.refs_1_ = f32[56,8,128]{2,1,0:T(8,128)S(1)} collective-permute-done((f32[56,8,128]{2,1,0:T(8,128)S(1)}, f32[56,8,128]{2,1,0:T(8,128)S(1)}, u32[]{:S(2)}, u32[]{:S(2)}) %collective-permute-start.13) | collective-permute-done | bytes 229408 | tf_op jit(solution)/shard_map/ppermute | solution.py:356
  109.9 6.1 %collective-permute-done.14.refs_7_.refs_2_ = f32[56,8,128]{2,1,0:T(8,128)S(1)} collective-permute-done((f32[56,8,128]{2,1,0:T(8,128)S(1)}, f32[56,8,128]{2,1,0:T(8,128)S(1)}, u32[]{:S(2)}, u32[]{:S(2)}) %collective-permute-start.14) | collective-permute-done | bytes 229408 | tf_op jit(solution)/shard_map/ppermute | solution.py:356
  116.0 1.4 shard_map.30
  117.4 0.1 collective-permute-start.18
  117.5 2.9 %collective-permute-done.18.refs_1_ = f32[4,75,8,128]{3,2,1,0:T(8,128)S(1)} collective-permute-done((f32[4,75,8,128]{3,2,1,0:T(8,128)S(1)}, f32[4,75,8,128]{3,2,1,0:T(8,128)S(1)}, u32[]{:S(2)}, u32[]{:S(2)}) %collective-permute-start.18) | collective-permute-done | bytes 1228832 | tf_op jit(solution)/shard_map/ppermute | solution.py:339
  120.4 0.2 shard_map.31
  120.6 24.2 %all_to_all.15.refs_4_ = f32[4,75,8,128]{3,2,1,0:T(8,128)S(1)} all-to-all(f32[4,75,8,128]{3,2,1,0:T(8,128)S(1)} %shard_map.31), channel_id=1, replica_groups=mesh['x'=4,'zl'=4,'y'=4,'zh'=2,'c'=2] {'y'}, dimensions={0} | all-to-all | bytes 2457600 | tf_op jit(solution)/shard_map/all_to_all | solution.py:368
  144.8 0.1 shard_map.32
  144.9 18.5 %all_to_all.16.part_ref = f32[4,41,8,128]{3,2,1,0:T(8,128)S(1)} all-to-all(f32[4,41,8,128]{3,2,1,0:T(8,128)S(1)} %shard_map.32), channel_id=1, replica_groups=mesh['x'=4,'zl'=4,'y'=4,'zh'=2,'c'=2] {'x'}, dimensions={0} | all-to-all | bytes 1343488 | tf_op jit(solution)/shard_map/all_to_all | solution.py:377
  163.4 0.5 shard_map.33
  164.0 13.6 %all_to_all.17.part_ref = f32[8,6,8,128]{3,2,1,0:T(8,128)S(1)} all-to-all(f32[8,6,8,128]{3,2,1,0:T(8,128)S(1)} %shard_map.33), channel_id=1, replica_groups=mesh['x'=4,'zl'=4,'y'=4,'zh'=2,'c'=2] {'zl','zh'}, dimensions={0} | all-to-all | bytes 393216 | tf_op jit(solution)/shard_map/all_to_all | solution.py:386
  177.5 1.0 shard_map.34
  (14 shorter events, 0.1 us)
Async XLA Ops:
  4.6 5.3 %collective-permute-start.1 = (f32[256,128]{1,0:T(8,128)}, f32[256,128]{1,0:T(8,128)S(1)}, u32[]{:S(2)}, u32[]{:S(2)}) collective-permute-start(f32[256,128]{1,0:T(8,128)} %get-tuple-element.41.order_ref), channel_id=1, source_target_pairs={{1,0},{2,1},{3,2},{4,3},{5,4},{6,5},{7,6},{8,7},{9,8},{10,9},{11,1... | collective-permute-start | bytes 393224 | tf_op jit(solution)/shard_map/ppermute | solution.py:288
  5.9 4.2 %collective-permute-start = (f32[256,128]{1,0:T(8,128)}, f32[256,128]{1,0:T(8,128)S(1)}, u32[]{:S(2)}, u32[]{:S(2)}) collective-permute-start(f32[256,128]{1,0:T(8,128)} %get-tuple-element.40), channel_id=1, source_target_pairs={{0,1},{1,2},{2,3},{3,4},{4,5},{5,6},{6,7},{7,8},{8,9},{9,10},{10,1... | collective-permute-start | bytes 393224 | tf_op jit(solution)/shard_map/ppermute | solution.py:288
  8.9 0.9 copy-start
  13.1 21.7 %collective-permute-start.3 = (f32[4,256,128]{2,1,0:T(8,128)S(1)}, f32[4,256,128]{2,1,0:T(8,128)S(1)}, u32[]{:S(2)}, u32[]{:S(2)}) collective-permute-start(f32[4,256,128]{2,1,0:T(8,128)S(1)} %get-tuple-element.43.order_ref.top_ref), channel_id=1, source_target_pairs={{16,0},{32,16},{48,32},{64,48},{80,64},{96,80},{112,96},{128,112},... | collective-permute-start | bytes 1572872 | tf_op jit(solution)/shard_map/ppermute | solution.py:288
  16.9 25.6 %collective-permute-start.2 = (f32[4,256,128]{2,1,0:T(8,128)S(1)}, f32[4,256,128]{2,1,0:T(8,128)S(1)}, u32[]{:S(2)}, u32[]{:S(2)}) collective-permute-start(f32[4,256,128]{2,1,0:T(8,128)S(1)} %get-tuple-element.42.bot_ref), channel_id=1, source_target_pairs={{0,16},{16,32},{32,48},{48,64},{64,80},{80,96},{96,112},{112,128},... | collective-permute-start | bytes 1572872 | tf_op jit(solution)/shard_map/ppermute | solution.py:288
  22.1 28.7 %collective-permute-start.5 = (f32[4,256,128]{2,1,0:T(8,128)S(1)}, f32[4,256,128]{2,1,0:T(8,128)S(1)}, u32[]{:S(2)}, u32[]{:S(2)}) collective-permute-start(f32[4,256,128]{2,1,0:T(8,128)S(1)} %get-tuple-element.44.order_ref.top_ref), channel_id=1, source_target_pairs={{16,0},{32,16},{48,32},{64,48},{80,64},{96,80},{112,96},{128,112},... | collective-permute-start | bytes 1572872 | tf_op jit(solution)/shard_map/ppermute | solution.py:288
  25.9 24.9 %collective-permute-start.4 = (f32[4,256,128]{2,1,0:T(8,128)S(1)}, f32[4,256,128]{2,1,0:T(8,128)S(1)}, u32[]{:S(2)}, u32[]{:S(2)}) collective-permute-start(f32[4,256,128]{2,1,0:T(8,128)S(1)} %get-tuple-element.48.bot_ref), channel_id=1, source_target_pairs={{0,16},{16,32},{32,48},{48,64},{64,80},{80,96},{96,112},{112,128},... | collective-permute-start | bytes 1572872 | tf_op jit(solution)/shard_map/ppermute | solution.py:288
  31.0 46.1 %collective-permute-start.8 = (f32[4,256,128]{2,1,0:T(8,128)S(1)}, f32[4,256,128]{2,1,0:T(8,128)S(1)}, u32[]{:S(2)}, u32[]{:S(2)}) collective-permute-start(f32[4,256,128]{2,1,0:T(8,128)S(1)} %get-tuple-element.45.order_ref.top_ref), channel_id=1, source_target_pairs={{16,0},{32,16},{48,32},{64,48},{80,64},{96,80},{112,96},{128,112},... | collective-permute-start | bytes 1572872 | tf_op jit(solution)/shard_map/ppermute | solution.py:288
  34.8 42.3 %collective-permute-start.7 = (f32[4,256,128]{2,1,0:T(8,128)S(1)}, f32[4,256,128]{2,1,0:T(8,128)S(1)}, u32[]{:S(2)}, u32[]{:S(2)}) collective-permute-start(f32[4,256,128]{2,1,0:T(8,128)S(1)} %get-tuple-element.52.bot_ref), channel_id=1, source_target_pairs={{0,16},{16,32},{32,48},{48,64},{64,80},{80,96},{96,112},{112,128},... | collective-permute-start | bytes 1572872 | tf_op jit(solution)/shard_map/ppermute | solution.py:288
  52.7 39.9 %collective-permute-start.6 = (f32[4,32,8,128]{3,2,1,0:T(8,128)S(1)}, f32[4,32,8,128]{3,2,1,0:T(8,128)S(1)}, u32[]{:S(2)}, u32[]{:S(2)}) collective-permute-start(f32[4,32,8,128]{3,2,1,0:T(8,128)S(1)} %get-tuple-element.51), channel_id=1, source_target_pairs={{0,1},{1,0},{2,3},{3,2},{4,5},{5,4},{6,7},{7,6},{8,9},{9,8},{10,11... | collective-permute-start | bytes 1572872 | tf_op jit(solution)/shard_map/ppermute | solution.py:339
  71.2 35.2 %collective-permute-start.17 = (f32[4,256,128]{2,1,0:T(8,128)S(1)}, f32[4,256,128]{2,1,0:T(8,128)S(1)}, u32[]{:S(2)}, u32[]{:S(2)}) collective-permute-start(f32[4,256,128]{2,1,0:T(8,128)S(1)} %get-tuple-element.46.refs_0_.top_ref), channel_id=1, source_target_pairs={{16,0},{32,16},{48,32},{64,48},{80,64},{96,80},{112,96},{128,112},... | collective-permute-start | bytes 1572872 | tf_op jit(solution)/shard_map/ppermute | solution.py:288
  73.2 33.3 %collective-permute-start.16 = (f32[4,256,128]{2,1,0:T(8,128)S(1)}, f32[4,256,128]{2,1,0:T(8,128)S(1)}, u32[]{:S(2)}, u32[]{:S(2)}) collective-permute-start(f32[4,256,128]{2,1,0:T(8,128)S(1)} %get-tuple-element.63.bot_ref), channel_id=1, source_target_pairs={{0,16},{16,32},{32,48},{48,64},{64,80},{80,96},{96,112},{112,128},... | collective-permute-start | bytes 1572872 | tf_op jit(solution)/shard_map/ppermute | solution.py:288
  78.9 12.0 %collective-permute-start.10 = (f32[4,6,8,128]{3,2,1,0:T(8,128)S(1)}, f32[4,6,8,128]{3,2,1,0:T(8,128)S(1)}, u32[]{:S(2)}, u32[]{:S(2)}) collective-permute-start(f32[4,6,8,128]{3,2,1,0:T(8,128)S(1)} %get-tuple-element.56), channel_id=1, source_target_pairs={{0,1},{1,0},{2,3},{3,2},{4,5},{5,4},{6,7},{7,6},{8,9},{9,8},{10,11... | collective-permute-start | bytes 294920 | tf_op jit(solution)/shard_map/ppermute | solution.py:339
  90.0 1.3 collective-permute-start.11
  91.0 1.3 collective-permute-start.12
  91.3 1.3 collective-permute-start.9
  92.7 17.1 %collective-permute-start.13 = (f32[56,8,128]{2,1,0:T(8,128)S(1)}, f32[56,8,128]{2,1,0:T(8,128)S(1)}, u32[]{:S(2)}, u32[]{:S(2)}) collective-permute-start(f32[56,8,128]{2,1,0:T(8,128)S(1)} %get-tuple-element.60), channel_id=1, source_target_pairs={{0,4},{4,8},{8,12},{12,0},{1,5},{5,9},{9,13},{13,1},{2,6},{6,10},{... | collective-permute-start | bytes 688136 | tf_op jit(solution)/shard_map/ppermute | solution.py:356
  102.1 13.8 %collective-permute-start.14 = (f32[56,8,128]{2,1,0:T(8,128)S(1)}, f32[56,8,128]{2,1,0:T(8,128)S(1)}, u32[]{:S(2)}, u32[]{:S(2)}) collective-permute-start(f32[56,8,128]{2,1,0:T(8,128)S(1)} %get-tuple-element.61), channel_id=1, source_target_pairs={{0,8},{4,12},{8,0},{12,4},{1,9},{5,13},{9,1},{13,5},{2,10},{6,14},... | collective-permute-start | bytes 688136 | tf_op jit(solution)/shard_map/ppermute | solution.py:356
  105.3 10.6 %collective-permute-start.15 = (f32[56,8,128]{2,1,0:T(8,128)S(1)}, f32[56,8,128]{2,1,0:T(8,128)S(1)}, u32[]{:S(2)}, u32[]{:S(2)}) collective-permute-start(f32[56,8,128]{2,1,0:T(8,128)S(1)} %get-tuple-element.62), channel_id=1, source_target_pairs={{0,12},{4,0},{8,4},{12,8},{1,13},{5,1},{9,5},{13,9},{2,14},{6,2},{... | collective-permute-start | bytes 688136 | tf_op jit(solution)/shard_map/ppermute | solution.py:356
  117.4 3.0 %collective-permute-start.18 = (f32[4,75,8,128]{3,2,1,0:T(8,128)S(1)}, f32[4,75,8,128]{3,2,1,0:T(8,128)S(1)}, u32[]{:S(2)}, u32[]{:S(2)}) collective-permute-start(f32[4,75,8,128]{3,2,1,0:T(8,128)S(1)} %get-tuple-element.74), channel_id=1, source_target_pairs={{0,1},{1,0},{2,3},{3,2},{4,5},{5,4},{6,7},{7,6},{8,9},{9,8},{10,11... | collective-permute-start | bytes 3686408 | tf_op jit(solution)/shard_map/ppermute | solution.py:339
